TPU v7x, 128 devices: a whole 4x4x4 slice. The times are simulated.
128 devices in a mesh: dp: 8 (over z, core), expert: 16 (over x, y).
Axes of the slice: x: 4, y: 4, z: 4, core: 2. Of those that a mesh axis runs over, the one named last changes fastest.
Arguments:
- hidden_in: bfloat16 [16384, 1024], P(('dp', 'expert')), may hold values from -6 to 6
- routes: int32 [16384, 8], P(('dp', 'expert')), may hold values from 0 to 31, all different within a row
- first_gain: bfloat16 [1024], replicated, may hold values from 0.099609375 to 1.8984375
- query_weight: bfloat16 [1024, 1024], replicated, may hold values from -0.625 to 0.625
- key_weight: bfloat16 [1024, 512], replicated, may hold values from -0.625 to 0.625
- value_weight: bfloat16 [1024, 512], replicated, may hold values from -0.1875 to 0.1875
- output_weight: bfloat16 [1024, 1024], replicated, may hold values from -1 to 1
- second_gain: bfloat16 [1024], replicated, may hold values from 0.099609375 to 1.8984375
- router_weight: bfloat16 [1024, 32], replicated, may hold values from -0.09375 to 0.09375
- gateup_weight: bfloat16 [32, 1024, 1024], P('expert'), may hold values from -0.1875 to 0.1875
- down_weight: bfloat16 [32, 512, 1024], P('expert'), may hold values from -1 to 1
- cotangent: bfloat16 [16384, 1024], P(('dp', 'expert')), may hold values from -6 to 6
Outputs:
- layer_out: bfloat16 [16384, 1024], P(('dp', 'expert'))
- hidden_grad: bfloat16 [16384, 1024], P(('dp', 'expert'))
- gateup_grad: float32 [32, 1024, 1024], P('expert')
- down_grad: float32 [32, 512, 1024], P('expert')
- query_grad: float32 [1024, 1024], replicated
- key_grad: float32 [1024, 512], replicated
- value_grad: float32 [1024, 512], replicated
- output_grad: float32 [1024, 1024], replicated
- router_grad: float32 [1024, 32], replicated
- first_grad: float32 [1024], replicated
- second_grad: float32 [1024], replicated
Inputs may be any that keep to these rules, and one draw needn't show every extreme that they name: `routes`: each row names 8 different experts, and every expert is named by some row.
All inputs are finite; a program needn't handle non-finite values.
Results may differ from a plain program's by a relative error of at most 0.025.
Values may be sent and summed in bfloat16 or wider, within the bound.
No kernel may reach another device: no remote copies, remote signals or barrier semaphores. Data moves between devices by JAX's collectives and lax.ppermute only.
A program may use at most 192 MiB of HBM per device.

v0:
```python
import jax
import jax.numpy as jnp
from jax import lax
from jax.sharding import PartitionSpec as P

D = 1024
H = 16
KV = 8
HD = 64
FF = 512
TOP = 8


epsilon = 1e-06
score_scale = 0.015625


def sent_together(arrays, axis, dim, along):
    ends, at = ([], 0)
    for a in arrays[:-1]:
        at += a.shape[along]
        ends.append(at)
    both = jnp.concatenate(arrays, axis=along)
    return tuple(jnp.split(lax.all_gather(both, axis, axis=dim, tiled=True), ends, axis=along))


def side_by_side(arrays, axis, dim, along):
    widths = [a.shape[along] for a in arrays]
    both = jnp.concatenate(arrays, axis=along)
    out = lax.psum_scatter(both, axis, scatter_dimension=dim, tiled=True)
    return tuple(jnp.split(out, [sum(widths[:k]) for k in range(1, len(widths))], axis=along))


def together(arrays, axis):
    flat, at, done = (jnp.concatenate([a.reshape(-1) for a in arrays]), 0, [])
    subtotal = lax.psum(flat, axis)
    for a in arrays:
        done.append(subtotal[at : at + a.size].reshape(a.shape))
        at += a.size
    return tuple(done)


def rope_tables(offset, amount):
    places = (offset + jnp.arange(amount)).astype(jnp.float32)
    inverse = 10000.0 ** (-jnp.arange(0, HD, 2).astype(jnp.float32) / HD)
    angles = places[:, None] * inverse[None, :]
    return (jnp.cos(angles), jnp.sin(angles))


def rotate(values, cosine_table, sine_table):
    middle = values.shape[-1] // 2
    former, latter = (values[..., :middle], values[..., middle:])
    cosine_cols, sine_cols = (cosine_table[:, None, :], sine_table[:, None, :])
    return jnp.concatenate(
        [former * cosine_cols - latter * sine_cols, latter * cosine_cols + former * sine_cols], -1
    )


def rotate_back(gradient, cosine_table, sine_table):
    middle = gradient.shape[-1] // 2
    former, latter = (gradient[..., :middle], gradient[..., middle:])
    cosine_cols, sine_cols = (cosine_table[:, None, :], sine_table[:, None, :])
    return jnp.concatenate(
        [former * cosine_cols + latter * sine_cols, latter * cosine_cols - former * sine_cols], -1
    )


def inverse_rms(values):
    return lax.rsqrt(jnp.mean(values * values, -1, keepdims=True) + epsilon)


def norm_back(values, scale_rows, gain_row, grad_normed):
    scaled = grad_normed * gain_row
    grad_gain = jnp.sum(grad_normed * values * scale_rows, 0)
    grad_values = scale_rows * scaled - values * scale_rows**3 * jnp.mean(
        scaled * values, -1, keepdims=True
    )
    return (grad_values, grad_gain)


def score_block(query_rot, key_piece, first_key, first_query):
    key_heads = key_piece.reshape(key_piece.shape[0], KV, HD)
    raw_scores = (
        jnp.einsum("qkgd,nkd->kgqn", query_rot, key_heads, preferred_element_type=jnp.float32)
        * score_scale
    )
    query_places = first_query + jnp.arange(query_rot.shape[0])
    key_places = first_key + jnp.arange(key_piece.shape[0])
    visible = key_places[None, :] <= query_places[:, None]
    return jnp.where(visible, jnp.exp(raw_scores), 0.0)


def on_device(
    hidden_in,
    routes,
    first_gain,
    query_weight,
    key_weight,
    value_weight,
    output_weight,
    second_gain,
    router_weight,
    gateup_weight,
    down_weight,
    cotangent,
):
    row_count = hidden_in.shape[0]
    groups = H // KV
    first_query = lax.axis_index("expert") * row_count
    cosine_table, sine_table = rope_tables(first_query, row_count)
    hidden = hidden_in.astype(jnp.float32)
    gain_one = first_gain.astype(jnp.float32)
    scale_one = inverse_rms(hidden)
    normed_one = (hidden * scale_one * gain_one).astype(jnp.bfloat16)
    query_pre = jnp.dot(normed_one, query_weight, preferred_element_type=jnp.float32)
    key_pre = jnp.dot(normed_one, key_weight, preferred_element_type=jnp.float32)
    value_rows = jnp.dot(normed_one, value_weight, preferred_element_type=jnp.float32).astype(
        jnp.bfloat16
    )
    query_rot = (
        rotate(query_pre.reshape(row_count, H, HD), cosine_table, sine_table)
        .astype(jnp.bfloat16)
        .reshape(row_count, KV, groups, HD)
    )
    key_rot = (
        rotate(key_pre.reshape(row_count, KV, HD), cosine_table, sine_table)
        .astype(jnp.bfloat16)
        .reshape(row_count, KV * HD)
    )
    key_total = row_count * lax.axis_size("expert")
    key_block = min(512, key_total)
    block_count = (first_query + row_count + key_block - 1) // key_block

    def fold_keys(running, pieces, first_key):

        def include(current):
            weights = score_block(query_rot, pieces[0], first_key, first_query)
            value_heads = pieces[1].reshape(pieces[1].shape[0], KV, HD)
            added = jnp.einsum(
                "kgqn,nkd->kgqd",
                weights.astype(jnp.bfloat16),
                value_heads,
                preferred_element_type=jnp.float32,
            )
            return (current[0] + jnp.sum(weights, -1), current[1] + added)

        def unchanged(current):
            return current

        return lax.cond(first_key < first_query + row_count, include, unchanged, running)

    initial = (
        jnp.zeros((KV, groups, row_count), jnp.float32),
        jnp.zeros((KV, groups, row_count, HD), jnp.float32),
    )
    keys_all, values_all = sent_together((key_rot, value_rows), "expert", 0, 1)

    def local_step(step_index, current):
        first_key = step_index * key_block
        pieces = (
            lax.dynamic_slice_in_dim(keys_all, first_key, key_block, 0),
            lax.dynamic_slice_in_dim(values_all, first_key, key_block, 0),
        )
        return fold_keys(current, pieces, first_key)

    totals, mixture = lax.fori_loop(0, block_count, local_step, initial)
    attended = mixture / totals[..., None]
    attended_low = (
        jnp.transpose(attended, (2, 0, 1, 3)).reshape(row_count, H * HD).astype(jnp.bfloat16)
    )
    middle = hidden + jnp.dot(attended_low, output_weight, preferred_element_type=jnp.float32)
    gain_two = second_gain.astype(jnp.float32)
    scale_two = inverse_rms(middle)
    normed_two = (middle * scale_two * gain_two).astype(jnp.bfloat16)
    logits = jnp.dot(normed_two, router_weight, preferred_element_type=jnp.float32)
    experts_total = router_weight.shape[1]
    capacity = 2 * row_count * TOP // experts_total
    chosen_mask = routes[:, :, None] == jnp.arange(experts_total)[None, None, :]
    mask_float = chosen_mask.astype(jnp.float32)
    chosen = jnp.sum(mask_float * logits[:, None, :], -1)
    gate_prob = jax.nn.softmax(chosen, -1)
    counts = chosen_mask.astype(jnp.int32).reshape(row_count * TOP, experts_total)
    earlier = jnp.cumsum(counts, 0) - counts
    slot_rank = jnp.sum(earlier * counts, -1)
    retained = slot_rank < capacity
    target = jnp.where(
        retained, routes.reshape(-1) * capacity + slot_rank, experts_total * capacity
    )
    retained_float = retained.reshape(row_count, TOP).astype(jnp.float32)
    gate_used = gate_prob * retained_float
    outgoing = (
        jnp.zeros((experts_total * capacity, D), jnp.bfloat16)
        .at[target]
        .set(jnp.repeat(normed_two, TOP, 0), mode="drop")
    )
    arrived = lax.all_to_all(
        outgoing.reshape(experts_total, capacity, D),
        "expert",
        split_axis=0,
        concat_axis=1,
        tiled=True,
    )
    gate_up = jnp.einsum("ecd,edf->ecf", arrived, gateup_weight, preferred_element_type=jnp.float32)
    gate_part, up_part = (gate_up[..., :FF], gate_up[..., FF:])
    activated = (jax.nn.silu(gate_part) * up_part).astype(jnp.bfloat16)
    expert_out = jnp.einsum(
        "ecf,efd->ecd", activated, down_weight, preferred_element_type=jnp.float32
    ).astype(jnp.bfloat16)
    returned = lax.all_to_all(
        expert_out, "expert", split_axis=1, concat_axis=0, tiled=True
    ).reshape(experts_total * capacity, D)
    pair_rows = (
        jnp.take(returned, target, axis=0, mode="fill", fill_value=0)
        .astype(jnp.float32)
        .reshape(row_count, TOP, D)
    )
    layer_out = (middle + jnp.sum(gate_used[..., None] * pair_rows, 1)).astype(jnp.bfloat16)
    grad_out = cotangent.astype(jnp.float32)
    grad_gate = jnp.sum(pair_rows * grad_out[:, None, :], -1) * retained_float
    pair_grad = (
        (gate_used[..., None] * grad_out[:, None, :])
        .astype(jnp.bfloat16)
        .reshape(row_count * TOP, D)
    )
    grad_outgoing = (
        jnp.zeros((experts_total * capacity, D), jnp.bfloat16)
        .at[target]
        .set(pair_grad, mode="drop")
    )
    grad_expert = lax.all_to_all(
        grad_outgoing.reshape(experts_total, capacity, D),
        "expert",
        split_axis=0,
        concat_axis=1,
        tiled=True,
    )
    grad_active = jnp.einsum(
        "ecd,efd->ecf", grad_expert, down_weight, preferred_element_type=jnp.float32
    )
    down_grad = jnp.einsum(
        "ecf,ecd->efd", activated, grad_expert, preferred_element_type=jnp.float32
    )
    sigmoid_gate = jax.nn.sigmoid(gate_part)
    grad_gatepart = grad_active * up_part * sigmoid_gate * (1.0 + gate_part * (1.0 - sigmoid_gate))
    grad_uppart = grad_active * gate_part * sigmoid_gate
    grad_both = jnp.concatenate([grad_gatepart, grad_uppart], -1).astype(jnp.bfloat16)
    gateup_grad = jnp.einsum("ecd,ecf->edf", arrived, grad_both, preferred_element_type=jnp.float32)
    grad_arrived = jnp.einsum(
        "ecf,edf->ecd", grad_both, gateup_weight, preferred_element_type=jnp.float32
    )
    grad_returned = (
        lax.all_to_all(
            grad_arrived.astype(jnp.bfloat16), "expert", split_axis=1, concat_axis=0, tiled=True
        )
        .astype(grad_arrived.dtype)
        .reshape(experts_total * capacity, D)
    )
    grad_normed_two = jnp.sum(
        jnp.take(grad_returned, target, axis=0, mode="fill", fill_value=0).reshape(
            row_count, TOP, D
        ),
        1,
    )
    grad_chosen = gate_prob * (grad_gate - jnp.sum(gate_prob * grad_gate, -1, keepdims=True))
    grad_logits = jnp.sum(mask_float * grad_chosen[..., None], 1).astype(jnp.bfloat16)
    router_grad = jnp.dot(normed_two.T, grad_logits, preferred_element_type=jnp.float32)
    grad_normed_two = grad_normed_two + jnp.dot(
        grad_logits, router_weight.T, preferred_element_type=jnp.float32
    )
    grad_middle, second_grad = norm_back(middle, scale_two, gain_two, grad_normed_two)
    grad_middle = grad_out + grad_middle
    grad_middle_low = grad_middle.astype(jnp.bfloat16)
    output_grad = jnp.dot(attended_low.T, grad_middle_low, preferred_element_type=jnp.float32)
    grad_attended = jnp.dot(grad_middle_low, output_weight.T, preferred_element_type=jnp.float32)
    grad_attended = jnp.transpose(grad_attended.reshape(row_count, KV, groups, HD), (1, 2, 0, 3))
    delta = jnp.sum(grad_attended * attended, -1) / totals
    grad_mixture = (grad_attended / totals[..., None]).astype(jnp.bfloat16)

    def back_step(step_index, current):
        grad_query, grad_keys, grad_values = current
        first_key = step_index * key_block
        key_piece = lax.dynamic_slice_in_dim(keys_all, first_key, key_block, 0)
        value_piece = lax.dynamic_slice_in_dim(values_all, first_key, key_block, 0)
        weights = score_block(query_rot, key_piece, first_key, first_query)
        key_heads = key_piece.reshape(key_block, KV, HD)
        value_heads = value_piece.reshape(key_block, KV, HD)
        grad_weights = jnp.einsum(
            "kgqd,nkd->kgqn", grad_mixture, value_heads, preferred_element_type=jnp.float32
        )
        grad_scores = (weights * (grad_weights - delta[..., None])).astype(jnp.bfloat16)
        grad_query = grad_query + jnp.einsum(
            "kgqn,nkd->qkgd", grad_scores, key_heads, preferred_element_type=jnp.float32
        )
        key_part = jnp.einsum(
            "kgqn,qkgd->nkd", grad_scores, query_rot, preferred_element_type=jnp.float32
        )
        value_part = jnp.einsum(
            "kgqn,kgqd->nkd",
            weights.astype(jnp.bfloat16),
            grad_mixture,
            preferred_element_type=jnp.float32,
        )
        grad_keys = lax.dynamic_update_slice_in_dim(
            grad_keys, key_part.reshape(key_block, KV * HD), first_key, 0
        )
        grad_values = lax.dynamic_update_slice_in_dim(
            grad_values, value_part.reshape(key_block, KV * HD), first_key, 0
        )
        return (grad_query, grad_keys, grad_values)

    start_state = (
        jnp.zeros((row_count, KV, groups, HD), jnp.float32),
        jnp.zeros((key_total, KV * HD), jnp.float32),
        jnp.zeros((key_total, KV * HD), jnp.float32),
    )
    grad_query, grad_keys, grad_values = lax.fori_loop(0, block_count, back_step, start_state)
    key_sum, value_sum = tuple(
        (
            part.astype(jnp.float32)
            for part in side_by_side(
                ((grad_keys * score_scale).astype(jnp.bfloat16), grad_values.astype(jnp.bfloat16)),
                "expert",
                0,
                1,
            )
        )
    )
    grad_query_rot = grad_query.reshape(row_count, H, HD) * score_scale
    grad_query_low = (
        rotate_back(grad_query_rot, cosine_table, sine_table)
        .reshape(row_count, H * HD)
        .astype(jnp.bfloat16)
    )
    grad_key_low = (
        rotate_back(key_sum.reshape(row_count, KV, HD), cosine_table, sine_table)
        .reshape(row_count, KV * HD)
        .astype(jnp.bfloat16)
    )
    grad_value_low = value_sum.astype(jnp.bfloat16)
    query_grad = jnp.dot(normed_one.T, grad_query_low, preferred_element_type=jnp.float32)
    key_grad = jnp.dot(normed_one.T, grad_key_low, preferred_element_type=jnp.float32)
    value_grad = jnp.dot(normed_one.T, grad_value_low, preferred_element_type=jnp.float32)
    grad_normed_one = jnp.dot(grad_query_low, query_weight.T, preferred_element_type=jnp.float32)
    grad_normed_one = grad_normed_one + jnp.dot(
        grad_key_low, key_weight.T, preferred_element_type=jnp.float32
    )
    grad_normed_one = grad_normed_one + jnp.dot(
        grad_value_low, value_weight.T, preferred_element_type=jnp.float32
    )
    grad_hidden, first_grad = norm_back(hidden, scale_one, gain_one, grad_normed_one)
    hidden_grad = (grad_middle + grad_hidden).astype(jnp.bfloat16)
    first_grad, query_grad, key_grad, value_grad, output_grad, router_grad, second_grad = lax.psum(
        (first_grad, query_grad, key_grad, value_grad, output_grad, router_grad, second_grad),
        ("dp", "expert"),
    )
    gateup_grad, down_grad = tuple(
        (
            part.astype(jnp.float32)
            for part in together(
                (gateup_grad.astype(jnp.bfloat16), down_grad.astype(jnp.bfloat16)), "dp"
            )
        )
    )
    return (
        layer_out,
        hidden_grad,
        gateup_grad,
        down_grad,
        query_grad,
        key_grad,
        value_grad,
        output_grad,
        router_grad,
        first_grad,
        second_grad,
    )


def solution(mesh):
    placed = (
        P(("dp", "expert"), None),
        P(("dp", "expert"), None),
        P(),
        P(),
        P(),
        P(),
        P(),
        P(),
        P(),
        P("expert", None, None),
        P("expert", None, None),
        P(("dp", "expert"), None),
    )
    return jax.shard_map(
        on_device,
        mesh=mesh,
        in_specs=placed,
        out_specs=(
            P(("dp", "expert"), None),
            P(("dp", "expert"), None),
            P("expert", None, None),
            P("expert", None, None),
            P(),
            P(),
            P(),
            P(),
            P(),
            P(),
            P(),
        ),
        check_vma=False,
    )
```

profile of v0, /device:TPU:1, one launch (start us, length us, event | category | flops | bytes accessed | tf_op | source)
XLA Modules:
  0.0 791.9 jit_solution(4707332287071338780)
XLA Ops:
  15.0 9.0 %reduce-window.6 = s32[32,8,128]{2,1,0:T(8,128)S(1)} reduce-window(s32[32,8,128]{2,1,0:T(8,128)S(1)} %fusion.56, s32[]{:T(128)} %constant.128.clone.1), window={size=1x1x128 pad=0_0x0_0x127_0}, to_apply=%region_6.7 | reduce-window | flops 4161536 | bytes 262148 | tf_op jit(solution)/shard_map/reduce-window
  27.3 42.0 %all-gather.2.cloned.1.call-done = bf16[2048,1024]{1,0:T(8,128)(2,1)} async-done(((bf16[128,1024]{1,0:T(8,128)(2,1)}), bf16[2048,1024]{1,0:T(8,128)(2,1)}) %all-gather.2.cloned.1.call-update) | async-done | bytes 4194320 | tf_op jit(solution)/shard_map/all_gather | solution.py:24
  88.6 8.0 %scatter_custom_fusion = bf16[2048,1024]{1,0:T(8,128)(2,1)} fusion(s32[1024]{0:T(1024)S(1)} %bitcast.251, bf16[]{:T(256)} %constant.146.clone.1, bf16[128,1024]{1,0:T(8,128)(2,1)S(1)} %multiply_convert_fusion.4), kind=kCustom, calls=%fused_computation.62 | custom fusion | bytes 4456450 | tf_op jit(solution)/shard_map/scatter | solution.py:194
  96.5 64.5 %all_to_all.60 = bf16[32,64,1024]{2,1,0:T(8,128)(2,1)S(1)} all-to-all(bf16[32,64,1024]{2,1,0:T(8,128)(2,1)} %bitcast.224), channel_id=1, replica_groups=mesh['dp'=8,'expert'=16] {'expert'}, dimensions={0} | all-to-all | bytes 8388608 | tf_op jit(solution)/shard_map/all_to_all | solution.py:196
  161.6 8.1 %fusion.82 = f32[2,1024,1024]{1,2,0:T(8,128)S(1)} fusion(bf16[2,1024,1024]{2,1,0:T(8,128)(2,1)S(1)} %bitcast.229, bf16[2,1024,1024]{2,1,0:T(8,128)(2,1)} %param.27), kind=kOutput, calls=%fused_computation.171 | convolution fusion | flops 4294967296 | bytes 16777216 | tf_op jit(solution)/shard_map/ecd,edf->ecf/dot_general | solution.py:203
  178.9 8.5 %copy.129 = bf16[2,1024,1024]{2,0,1:T(2,128)(2,1)} copy(bf16[2,1024,1024]{2,1,0:T(8,128)(2,1)} %convolution_convert_fusion) | data formatting | bytes 8388608 | tf_op jit(solution)/shard_map/convert_element_type | solution.py:208
  196.8 46.8 %all-to-all-done.1 = bf16[2,1024,1024]{2,0,1:T(2,128)(2,1)} async-done(((bf16[2,1024,1024]{2,0,1:T(2,128)(2,1)}), bf16[2,1024,1024]{2,0,1:T(2,128)(2,1)}, u32[]{:S(2)}, u32[]{:S(2)}) %all-to-all-start.1) | async-done | bytes 4194336 | tf_op jit(solution)/shard_map/all_to_all | solution.py:209
  249.2 8.7 %gather_fusion = bf16[1024,1024]{1,0:T(8,128)(2,1)} fusion(bf16[2048,1024]{1,0:T(8,128)(2,1)} %bitcast.218, s32[1024]{0:T(1024)S(1)} %broadcast_clamp_fusion), kind=kCustom, calls=%fused_computation | custom fusion | bytes 4198400 | tf_op jit(solution)/shard_map/jit(_take)/gather | solution.py:213
  266.3 8.5 %scatter_custom_fusion.1 = bf16[2048,1024]{1,0:T(8,128)(2,1)} fusion(s32[1024]{0:T(1024)} %bitcast.253, f32[128,1024]{1,0:T(8,128)S(1)} %convert_element_type.181, f32[1024]{0:T(1024)S(1)} %compare_select_fusion.3, bf16[]{:T(256)} %constant.146.clone.1), kind=kCustom, calls=%fused_computation.59 | custom fusion | flops 2097152 | bytes 4723200 | tf_op jit(solution)/shard_map/scatter | solution.py:228
  283.1 45.4 %all-to-all-done.2 = bf16[32,64,1024]{2,1,0:T(8,128)(2,1)} async-done(((bf16[32,64,1024]{2,1,0:T(8,128)(2,1)}), bf16[32,64,1024]{2,1,0:T(8,128)(2,1)}, u32[]{:S(2)}, u32[]{:S(2)}) %all-to-all-start.2) | async-done | bytes 4194336 | tf_op jit(solution)/shard_map/all_to_all | solution.py:230
  331.4 7.4 multiply_convert_fusion.2
  342.4 8.5 %fusion.28 = bf16[2,1024,1024]{2,1,0:T(8,128)(2,1)} fusion(bf16[2,1024,1024]{2,1,0:T(8,128)(2,1)S(1)} %bitcast.230, bf16[2,1024,512]{1,2,0:T(8,128)(2,1)} %get-tuple-element.397, bf16[2,1024,512]{1,2,0:T(8,128)(2,1)S(1)} %copy-done.55), kind=kOutput, calls=%fused_computation.57 | convolution fusion | flops 4305453056 | bytes 12582912 | tf_op jit(solution)/shard_map/ecd,ecf->edf/dot_general | solution.py:247
  350.9 9.0 %fusion.27 = bf16[2,1024,1024]{2,1,0:T(8,128)(2,1)} fusion(bf16[2,1024,1024]{2,1,0:T(8,128)(2,1)S(1)} %copy-done.54, bf16[2,1024,512]{1,2,0:T(8,128)(2,1)} %get-tuple-element.397, bf16[2,1024,512]{1,2,0:T(8,128)(2,1)S(1)} %copy-done.55), kind=kOutput, calls=%fused_computation.56 | convolution fusion | flops 4305453056 | bytes 12582912 | tf_op jit(solution)/shard_map/ecf,edf->ecd/dot_general | solution.py:248
  359.9 8.5 %copy.134 = bf16[2,1024,1024]{2,0,1:T(2,128)(2,1)} copy(bf16[2,1024,1024]{2,1,0:T(8,128)(2,1)} %fusion.27) | data formatting | bytes 8388608 | tf_op jit(solution)/shard_map/convert_element_type | solution.py:253
  374.5 9.8 %all-to-all-start.3 = ((bf16[2,1024,1024]{2,0,1:T(2,128)(2,1)}), bf16[2,1024,1024]{2,0,1:T(2,128)(2,1)}, u32[]{:S(2)}, u32[]{:S(2)}) async-start(bf16[2,1024,1024]{2,0,1:T(2,128)(2,1)} %copy.134), calls=%async_computation.3 | async-start | bytes 8388608 | tf_op jit(solution)/shard_map/all_to_all | solution.py:252
  384.4 15.1 %pad_maximum_fusion = bf16[3145728]{0:T(1024)(128)(2,1)} fusion(bf16[1048576]{0:T(1024)(128)(2,1)S(1)} %bitcast.228, bf16[2097152]{0:T(1024)(128)(2,1)} %bitcast.221), kind=kLoop, calls=%fused_computation.38 | loop fusion | flops 12582912 | bytes 12582912 | tf_op jit(solution)/shard_map/concatenate | solution.py:35
  399.6 30.9 %all-to-all-done.3 = bf16[2,1024,1024]{2,0,1:T(2,128)(2,1)} async-done(((bf16[2,1024,1024]{2,0,1:T(2,128)(2,1)}), bf16[2,1024,1024]{2,0,1:T(2,128)(2,1)}, u32[]{:S(2)}, u32[]{:S(2)}) %all-to-all-start.3) | async-done | bytes 4194336 | tf_op jit(solution)/shard_map/all_to_all | solution.py:252
  437.7 10.2 %gather_fusion.1 = f32[1024,1024]{1,0:T(8,128)} fusion(f32[2048,1024]{1,0:T(8,128)} %bitcast.215, s32[1024]{0:T(1024)S(1)} %copy-done.40), kind=kCustom, calls=%fused_computation.1 | custom fusion | bytes 8392704 | tf_op jit(solution)/shard_map/jit(_take)/gather | solution.py:259
  458.1 10.4 %while.28 = (s32[]{:T(128)}, f32[128,8,2,64]{0,3,2,1:T(8,128)S(1)}, f32[2048,512]{0,1:T(8,128)}, bf16[2048,512]{0,1:T(8,128)(2,1)}, s32[]{:T(128)}, /*index=5*/b...) while((s32[]{:T(128)}, f32[128,8,2,64]{0,3,2,1:T(8,128)S(1)}, ...), condition=%wide.region_23.24_spmd, body=%wide.region_22.23_spmd.sunk | while | flops 679674496 | bytes 29570256 | solution.py:316
  480.6 8.0 %all-reduce.5.cloned.1.call-done = bf16[3145728]{0:T(1024)(128)(2,1)} async-done(((bf16[3145728]{0:T(1024)(128)(2,1)}), bf16[3145728]{0:T(1024)(128)(2,1)}) %all-reduce.5.cloned.1.call-update) | async-done | bytes 6291472 | tf_op jit(solution)/shard_map/psum | solution.py:36
  499.6 93.6 %reduce-scatter.4.cloned.1.call-done = bf16[128,1024]{1,0:T(8,128)(2,1)} async-done(((bf16[2048,1024]{1,0:T(8,128)(2,1)}), bf16[128,1024]{1,0:T(8,128)(2,1)}) %reduce-scatter.4.cloned.1.call-update) | async-done | bytes 262160
  606.9 9.4 %reshape.450 = f32[2,1024,1024]{2,1,0:T(8,128)} reshape(f32[2097152]{0:T(1024)} %slice_convert_fusion) | data formatting | bytes 16777216 | tf_op jit(solution)/shard_map/convert_element_type | solution.py:358
  620.1 66.8 %all-reduce = (f32[1024]{0:T(1024)}, f32[1024]{0:T(1024)}) all-reduce(f32[1024]{0:T(1024)S(1)} %get-tuple-element.335, f32[1024]{0:T(1024)S(1)} %get-tuple-element.333), channel_id=1, replica_groups=mesh['dp'=8,'expert'=16] {'dp','expert'}, use_global_device_ids=true, to_apply=%region_33.34 | all-reduce | flops 2048 | bytes 16384 | tf_op jit(solution)/shard_map/psum | solution.py:352
  687.8 85.8 %all-reduce.7.cloned.1.call-done = (f32[1024,1024]{1,0:T(8,128)}, f32[1024,512]{1,0:T(8,128)}, f32[1024,512]{1,0:T(8,128)}, f32[1024,1024]{1,0:T(8,128)}, f32[1024,32]{0,1:T(8,128)}) async-done(((f32[1024,1024]{1,0:T(8,128)}, f32[1024,512]{1,0:T(8,128)}, f32[1024,512]{1,0:T(8,128)}, f32[1024,1024]{1,0:T(8,128)}, f32[1024,32]{0,1:T(8,128)}), (f32[1024,1024]{1,0:T(8,128)}, f32[1024,512]{1,0:T(8,128)}, ...) | async-done | bytes 12714000 | tf_op jit(solution)/shard_map/psum | solution.py:352
  (251 shorter events, 171.2 us)
Async XLA Ops:
  7.2 167.3 %copy-start = (bf16[2,512,1024]{2,1,0:T(8,128)(2,1)S(1)}, bf16[2,512,1024]{2,1,0:T(8,128)(2,1)}, u32[]{:S(2)}) copy-start(bf16[2,512,1024]{2,1,0:T(8,128)(2,1)} %param.28) | copy-start | bytes 6291460
  7.2 17.2 %copy-start.2 = (bf16[128,1024]{1,0:T(8,128)(2,1)S(1)}, bf16[128,1024]{1,0:T(8,128)(2,1)}, u32[]{:S(2)}) copy-start(bf16[128,1024]{1,0:T(8,128)(2,1)} %param.18) | copy-start | bytes 786436
  7.2 62.0 %all-gather.2.cloned.1.call-start = ((), (), s32[]{:S(2)}) async-start(), calls=%async_computation.5 | async-start | bytes 4456448 | tf_op jit(solution)/shard_map/all_gather | solution.py:24
  9.1 17.9 %copy-start.43 = (f32[128]{0:T(128)}, f32[128]{0:T(128)S(1)}, u32[]{:S(2)}) copy-start(f32[128]{0:T(128)S(1)} %get-tuple-element.417) | copy-start | bytes 1540
  9.8 17.2 %copy-start.30 = (f32[1024]{0:T(1024)}, f32[1024]{0:T(1024)S(1)}, u32[]{:S(2)}) copy-start(f32[1024]{0:T(1024)S(1)} %convert_element_type.164) | copy-start | bytes 12292
  13.5 60.2 %copy-start.26 = (f32[128,32]{0,1:T(8,128)}, f32[128,32]{0,1:T(8,128)S(1)}, u32[]{:S(2)}) copy-start(f32[128,32]{0,1:T(8,128)S(1)} %get-tuple-element.414) | copy-start | bytes 49156
  13.5 60.2 %copy-start.28 = (f32[128,32]{0,1:T(8,128)}, f32[128,32]{0,1:T(8,128)S(1)}, u32[]{:S(2)}) copy-start(f32[128,32]{0,1:T(8,128)S(1)} %get-tuple-element.415) | copy-start | bytes 49156
  27.3 165.1 %copy-start.37 = (s32[1024]{0:T(1024)}, s32[1024]{0:T(1024)S(1)}, u32[]{:S(2)}) copy-start(s32[1024]{0:T(1024)S(1)} %fusion.51) | copy-start | bytes 12292
  27.3 167.7 %copy-start.45 = (s32[1024,1]{0,1:T(1,128)}, s32[1024,1]{0,1:T(1,128)S(1)}, u32[]{:S(2)}) copy-start(s32[1024,1]{0,1:T(1,128)S(1)} %compare_select_fusion) | copy-start | bytes 12292
  88.2 72.9 %copy-start.48 = (f32[128]{0:T(128)}, f32[128]{0:T(128)S(1)}, u32[]{:S(2)}) copy-start(f32[128]{0:T(128)S(1)} %get-tuple-element.419) | copy-start | bytes 1540
  88.5 72.5 %copy-start.15 = (bf16[128,1024]{1,0:T(8,128)(2,1)}, bf16[128,1024]{1,0:T(8,128)(2,1)S(1)}, u32[]{:S(2)}) copy-start(bf16[128,1024]{1,0:T(8,128)(2,1)S(1)} %multiply_convert_fusion.4) | copy-start | bytes 786436
  187.4 56.2 %all-to-all-start.1 = ((bf16[2,1024,1024]{2,0,1:T(2,128)(2,1)}), bf16[2,1024,1024]{2,0,1:T(2,128)(2,1)}, u32[]{:S(2)}, u32[]{:S(2)}) async-start(bf16[2,1024,1024]{2,0,1:T(2,128)(2,1)} %copy.129), calls=%async_computation.1 | async-start | bytes 8388608 | tf_op jit(solution)/shard_map/all_to_all | solution.py:209
  195.0 54.2 %copy-start.39 = (s32[1024]{0:T(1024)}, s32[1024]{0:T(1024)S(1)}, u32[]{:S(2)}) copy-start(s32[1024]{0:T(1024)S(1)} %broadcast_clamp_fusion) | copy-start | bytes 12292
  196.2 53.0 %copy-start.38 = (f32[128,8]{0,1:T(8,128)}, f32[128,8]{0,1:T(8,128)S(1)}, u32[]{:S(2)}) copy-start(f32[128,8]{0,1:T(8,128)S(1)} %select_reduce_fusion.1) | copy-start | bytes 12292
  196.2 53.0 %copy-start.47 = (f32[128]{0:T(128)}, f32[128]{0:T(128)S(1)}, u32[]{:S(2)}) copy-start(f32[128]{0:T(128)S(1)} %reduce_max.9) | copy-start | bytes 1540
  274.8 53.6 %all-to-all-start.2 = ((bf16[32,64,1024]{2,1,0:T(8,128)(2,1)}), bf16[32,64,1024]{2,1,0:T(8,128)(2,1)}, u32[]{:S(2)}, u32[]{:S(2)}) async-start(bf16[32,64,1024]{2,1,0:T(8,128)(2,1)} %bitcast.222), calls=%async_computation.2 | async-start | bytes 8388608 | tf_op jit(solution)/shard_map/all_to_all | solution.py:230
  374.5 55.9 %all-to-all-start.3 = ((bf16[2,1024,1024]{2,0,1:T(2,128)(2,1)}), bf16[2,1024,1024]{2,0,1:T(2,128)(2,1)}, u32[]{:S(2)}, u32[]{:S(2)}) async-start(bf16[2,1024,1024]{2,0,1:T(2,128)(2,1)} %copy.134), calls=%async_computation.3 | async-start | bytes 8388608 | tf_op jit(solution)/shard_map/all_to_all | solution.py:252
  384.3 104.2 %all-reduce.5.cloned.1.call-start = ((), (), s32[]{:S(2)}) async-start(), calls=%async_computation.6 | async-start | bytes 12582912 | tf_op jit(solution)/shard_map/psum | solution.py:36
  399.5 193.6 %reduce-scatter.4.cloned.1.call-start = ((), (), s32[]{:S(2)}) async-start(), calls=%async_computation.7 | async-start | bytes 4456448
  480.5 13.6 %copy-start.3 = (bf16[128,1024]{1,0:T(8,128)(2,1)S(1)}, bf16[128,1024]{1,0:T(8,128)(2,1)}, u32[]{:S(2)}) copy-start(bf16[128,1024]{1,0:T(8,128)(2,1)} %param.18) | copy-start | bytes 786436
  480.5 13.6 %copy-start.31 = (f32[1024]{0:T(1024)S(1)}, f32[1024]{0:T(1024)}, u32[]{:S(2)}) copy-start(f32[1024]{0:T(1024)} %copy-done.30) | copy-start | bytes 12292
  480.5 13.6 %copy-start.44 = (f32[128]{0:T(128)S(1)}, f32[128]{0:T(128)}, u32[]{:S(2)}) copy-start(f32[128]{0:T(128)} %copy-done.43) | copy-start | bytes 1540
  480.5 293.0 %all-reduce.7.cloned.1.call-start = ((), (), s32[]{:S(2)}) async-start(), calls=%async_computation.8 | async-start | bytes 25427968 | tf_op jit(solution)/shard_map/psum | solution.py:352
  616.3 70.5 %copy-start.52 = (f32[128]{0:T(128)S(1)}, f32[128]{0:T(128)}, u32[]{:S(2)}) copy-start(f32[128]{0:T(128)} %get-tuple-element.416) | copy-start | bytes 1540
  (39 other events, 231.3 us)
Sparse Core Ops, SparseCore 0:
  14.6 54.6 all-gather.1
  399.6 88.8 all-reduce.4
  492.5 100.6 reduce-scatter.3
  601.2 172.3 all-reduce.6
where the time goes:
time: 802 us; the launch traced here: 792 us
  waiting for transfers between devices  352 us (44%)
  blocking collectives  131 us (16%)
  local copies, waits for them, and re-layouts  129 us (16%)
  matrix products  73.4 us (9%)
  other arithmetic  70.4 us (9%)
  starting transfers between devices  20.6 us (3%)
  between operations  15.1 us (2%)
    unnamed x5, waiting for transfers between devices  93.6 us
    psum x1, waiting for transfers between devices, on_device(): lax.psum((first_grad, query_grad, key_grad, value_grad, output_grad, rout...  85.8 us
    psum x1, blocking collectives, on_device(): lax.psum((first_grad, query_grad, key_grad, value_grad, output_grad, rout...  66.8 us
    all_to_all x1, blocking collectives, on_device(): lax.all_to_all(outgoing.reshape(experts_total, capacity, D), 'expert', sp...  64.5 us
    all_to_all x1, waiting for transfers between devices, on_device(): lax.all_to_all(expert_out, 'expert', split_axis=1, concat_axis=0, tiled=T...  46.8 us
    all_to_all x1, waiting for transfers between devices, on_device(): lax.all_to_all(grad_outgoing.reshape(experts_total, capacity, D), 'expert...  45.4 us
    all_gather x1, waiting for transfers between devices, sent_together(): lax.all_gather(both, axis, axis=dim, tiled=True)  42 us
    all_to_all x1, waiting for transfers between devices, on_device(): lax.all_to_all(grad_arrived.astype(jnp.bfloat16), 'expert', split_axis=1,...  30.9 us
  transfers between devices with their start and end apart: 7, of which 7 were waited for; matrix products, arithmetic and copies ran while one was open for 15% of the time, Pallas kernels for 0%

commit v1 on v0

v1 whole, which is shorter than its diff:
```python
import functools

import jax
import jax.numpy as jnp
from jax import lax
from jax.experimental import pallas as pl
from jax.experimental.pallas import tpu as pltpu
from jax.sharding import PartitionSpec as P

D = 1024
H = 16
KV = 8
HD = 64
FF = 512
TOP = 8
EXPERTS = 32
CAPACITY = 64
TOK = 128
SEQ = 2048

epsilon = 1e-06
score_scale = 0.015625

bf16 = jnp.bfloat16
f32 = jnp.float32
AXES = ("dp", "expert")

NT = (((1,), (1,)), ((), ()))
TN = (((0,), (0,)), ((), ()))


def dot(a, b):
    return jnp.dot(a, b, preferred_element_type=f32)


def dot_nt(a, b):
    return lax.dot_general(a, b, NT, preferred_element_type=f32)


def dot_tn(a, b):
    return lax.dot_general(a, b, TN, preferred_element_type=f32)


def moves(step):
    pairs = []
    for z in range(4):
        for c in range(2):
            for x in range(4):
                for y in range(4):
                    z2, c2, x2, y2 = step(z, c, x, y)
                    target = (((z2 % 4) * 2 + c2 % 2) * 4 + x2 % 4) * 4 + y2 % 4
                    pairs.append((((z * 2 + c) * 4 + x) * 4 + y, target))
    return pairs


def along_u(n):
    return moves(lambda z, c, x, y: (z, c, x, y + n) if c == 0 else (z, c, x + n, y))


def along_v(n):
    return moves(lambda z, c, x, y: (z, c, x + n, y) if c == 0 else (z, c, x, y + n))


def along_z(n):
    return moves(lambda z, c, x, y: (z + n, c, x, y))


def other_core():
    return moves(lambda z, c, x, y: (z, c + 1, x, y))


def pair_head():
    return moves(lambda z, c, x, y: (z, c, x, y ^ 1))


def send(array, pairs):
    return lax.ppermute(array, AXES, pairs)


def gather_axis(array, along):
    return [array] + [send(array, along(-n)) for n in (1, 2, 3)]


def sum_axis(parts, along):
    return [parts[0]] + [send(parts[n], along(n)) for n in (1, 2, 3)]


def added(parts):
    total = parts[0].astype(f32)
    for part in parts[1:]:
        total = total + part.astype(f32)
    return total


def call(body, outs, args, scratch=(), specs=None, flops=0, moved=0, limit=48, name=None):
    vmem = pl.BlockSpec(memory_space=pltpu.VMEM)
    return pl.pallas_call(
        body,
        out_shape=outs,
        in_specs=[vmem] * len(args) if specs is None else specs,
        out_specs=[vmem] * len(outs),
        scratch_shapes=list(scratch),
        compiler_params=pltpu.CompilerParams(vmem_limit_bytes=limit * 1024 * 1024),
        cost_estimate=pl.CostEstimate(flops=flops, bytes_accessed=moved, transcendentals=0),
        name=name,
    )(*args)


def shape(dims, kind=bf16):
    return jax.ShapeDtypeStruct(dims, kind)


def project_body(hid, gain, wq, wk, wv, cosine, sine, out, normed):
    hidden = hid[...].astype(f32)
    r1 = lax.rsqrt(jnp.mean(hidden * hidden, -1, keepdims=True) + epsilon)
    n1 = (hidden * r1 * gain[...]).astype(bf16)
    normed[...] = n1
    cos = cosine[...][None]
    sin = sine[...][None]

    def rotated(value, heads):
        value = value.T.reshape(heads, HD, TOK)
        a, b = value[:, : HD // 2], value[:, HD // 2 :]
        return jnp.concatenate([a * cos - b * sin, b * cos + a * sin], 1).astype(bf16)

    key = rotated(dot(n1, wk[...]), KV)
    value = dot(n1, wv[...]).T.reshape(KV, HD, TOK).astype(bf16)
    query = rotated(dot(n1, wq[...]), H)
    for h in range(H):
        out[h, 0:64] = query[h]
        out[h, 64:128] = key[h // 2]
        out[h, 128:192] = value[h // 2]


def attend_body(recv, att_send, att, totals, qkv):
    for s in range(16):
        qkv[:, 128 * s : 128 * s + 128] = recv[s]
    rows = lax.broadcasted_iota(jnp.int32, (256, 256), 0)
    cols = lax.broadcasted_iota(jnp.int32, (256, 256), 1)
    visible = rows <= cols
    for i in range(8):
        here = slice(256 * i, 256 * i + 256)
        query = qkv[0:64, here]
        weights = jnp.exp(dot_tn(qkv[64:128, here], query) * score_scale)
        weights = jnp.where(visible, weights, 0.0)
        total = jnp.sum(weights, 0, keepdims=True)
        mixture = dot(qkv[128:192, here], weights.astype(bf16))
        if i:
            before = slice(0, 256 * i)
            weights = jnp.exp(dot_tn(qkv[64:128, before], query) * score_scale)
            total = total + jnp.sum(weights, 0, keepdims=True)
            mixture = mixture + dot(qkv[128:192, before], weights.astype(bf16))
        mixed = mixture / total
        att[:, here] = mixed
        totals[:, here] = total
        att_send[2 * i] = mixed[:, :128].astype(bf16)
        att_send[2 * i + 1] = mixed[:, 128:].astype(bf16)


def middle_body(att_t, hid, wo, gain, middle, scale, normed):
    attended = att_t[...].reshape(D, TOK).T
    mid = hid[...].astype(f32) + dot(attended, wo[...])
    r2 = lax.rsqrt(jnp.mean(mid * mid, -1, keepdims=True) + epsilon)
    middle[...] = mid
    scale[...] = jnp.broadcast_to(r2, scale.shape)
    normed[...] = (mid * r2 * gain[...]).astype(bf16)


def expert_body(
    src, n2, cot, code, router, wgu, wd, part, x_out, g_out, act_out, gb_out, cot_v, wgu_v, wd_v, dx_v, sems
):
    copies = []
    for j in range(4):
        copies.append(pltpu.make_async_copy(cot.at[src[j], pl.ds(0, TOK)], cot_v.at[j], sems.at[j]))
    for e in range(2):
        copies.append(pltpu.make_async_copy(wgu.at[e], wgu_v.at[e], sems.at[4 + e]))
        copies.append(pltpu.make_async_copy(wd.at[e], wd_v.at[e], sems.at[6 + e]))
    for copy in copies:
        copy.start()
    slots = lax.broadcasted_iota(jnp.int32, (CAPACITY, TOK), 0).astype(f32)
    places = []
    gates = []
    for j in range(4):
        rows = n2[j]
        logits = dot_nt(router[...], rows)
        codes = code[src[j]]
        chosen = codes > -1.5
        top = jnp.max(jnp.where(chosen, logits, -1e30), 0, keepdims=True)
        powers = jnp.where(chosen, jnp.exp(logits - top), 0.0)
        prob = powers / jnp.sum(powers, 0, keepdims=True)
        where = [codes[e : e + 1] == slots for e in range(2)]
        places.append(jnp.concatenate([w.astype(f32) for w in where], 0).astype(bf16))
        gates.append([jnp.sum(jnp.where(where[e], prob[e : e + 1], 0.0), 1, keepdims=True) for e in range(2)])
        copies[j].wait()
        here = slice(64 * j, 64 * j + 64)
        picked = dot(places[j], rows).astype(bf16)
        x_out[0, here] = picked[:64]
        x_out[1, here] = picked[64:]
        picked = dot(places[j], cot_v[j]).astype(bf16)
        g_out[0, here] = picked[:64]
        g_out[1, here] = picked[64:]
    grad_gates = []
    for e in range(2):
        copies[4 + 2 * e].wait()
        copies[5 + 2 * e].wait()
        both = dot(x_out[e], wgu_v[e])
        active = dot_nt(g_out[e], wd_v[e])
        gate, up = both[:, :FF], both[:, FF:]
        s = 1.0 / (1.0 + jnp.exp(-gate))
        silu = gate * s
        act = silu * up
        weight = jnp.concatenate([gates[j][e] for j in range(4)], 0)
        act_out[e] = (act * weight).astype(bf16)
        grad_gates.append(jnp.sum(act * active, 1, keepdims=True))
        grad_active = active * weight
        gb_out[e, :, :FF] = (grad_active * up * s * (1.0 + gate * (1.0 - s))).astype(bf16)
        gb_out[e, :, FF:] = (grad_active * silu).astype(bf16)
        grad_x = dot_nt(gb_out[e], wgu_v[e]).astype(bf16)
        for j in range(4):
            dx_v[j, 64 * e : 64 * e + 64] = grad_x[64 * j : 64 * j + 64]
    first = src[4] * 2
    lane = lax.broadcasted_iota(jnp.int32, (16, D), 1) // TOK
    cell = lax.broadcasted_iota(jnp.int32, (16, D), 0) * 8 + lane
    for j in range(4):
        part[j, 0:TOK] = dot_tn(places[j], dx_v[j]).astype(bf16)
        tail = jnp.zeros((16, D), f32)
        for e in range(2):
            column = grad_gates[e][64 * j : 64 * j + 64]
            row = jnp.sum(places[j][64 * e : 64 * e + 64].astype(f32) * column, 0, keepdims=True)
            tail = jnp.where(cell == first + e, jnp.concatenate([row] * 8, 1), tail)
        part[j, TOK : TOK + 16] = tail.astype(bf16)


def expert_grad_body(*refs):
    x, g, act, gb = refs[0:4], refs[4:8], refs[8:12], refs[12:16]
    gu_out, down_out = refs[16:18]
    xs, gs, acts, gbs = refs[18:22]
    for i in range(4):
        here = slice(256 * i, 256 * i + 256)
        xs[here] = x[i][0]
        gs[here] = g[i][0]
        acts[here] = act[i][0]
        gbs[here] = gb[i][0]
    for b in range(4):
        here = slice(256 * b, 256 * b + 256)
        gu_out[0, here] = dot_tn(xs[:, here], gbs[...]).astype(bf16)
    for b in range(2):
        here = slice(256 * b, 256 * b + 256)
        down_out[0, here] = dot_tn(acts[:, here], gs[...]).astype(bf16)


def expert_result_body(src, act, code, wd, out, rows_v):
    slots = lax.broadcasted_iota(jnp.int32, (CAPACITY, TOK), 0).astype(f32)
    for e in range(2):
        result = dot(act[e], wd[e]).astype(bf16)
        for j in range(4):
            rows_v[j, 64 * e : 64 * e + 64] = result[64 * j : 64 * j + 64]
    for j in range(4):
        codes = code[src[j]]
        place = jnp.concatenate([(codes[e : e + 1] == slots).astype(f32) for e in range(2)], 0).astype(bf16)
        out[j] = dot_tn(place, rows_v[j]).astype(bf16)


def norm_back_body(
    p0, p1, p2, p3, n2, middle, scale, gain, cot, code, router, wo, grad_mid, low_mid, datt, router_grad, second
):
    total = added([p0[...], p1[...], p2[...], p3[...]])
    grad = total[:TOK]
    packed = total[TOK : TOK + 4]
    grad_gate = jnp.concatenate(
        [packed[k // 8 : k // 8 + 1, TOK * (k % 8) : TOK * (k % 8) + TOK] for k in range(EXPERTS)], 0
    )
    rows = n2[...]
    logits = dot_nt(router[...], rows)
    chosen = code[...] > -1.5
    top = jnp.max(jnp.where(chosen, logits, -1e30), 0, keepdims=True)
    powers = jnp.where(chosen, jnp.exp(logits - top), 0.0)
    prob = powers / jnp.sum(powers, 0, keepdims=True)
    grad_chosen = prob * (grad_gate - jnp.sum(prob * grad_gate, 0, keepdims=True))
    grad_logits = grad_chosen.astype(bf16)
    router_grad[...] = dot(grad_logits, rows)
    grad = grad + dot_tn(grad_logits, router[...])
    mid = middle[...]
    r2 = scale[:, 0:1]
    g2 = grad * gain[...]
    second[...] = jnp.sum(grad * mid * r2, 0, keepdims=True)
    grad_middle = cot[...].astype(f32) + r2 * g2 - mid * r2 * r2 * r2 * jnp.mean(g2 * mid, -1, keepdims=True)
    grad_mid[...] = grad_middle
    low = grad_middle.astype(bf16)
    low_mid[...] = low
    datt[...] = dot_nt(wo[...], low).astype(bf16).reshape(H, HD, TOK)


def output_grad_body(order, att, low, router_grad, second, out):
    grad = dot(att[...].reshape(D, TOK), low[...])
    for r in range(H):
        h = order[r]
        out[r, 64:80] = jnp.zeros((16, D), bf16)
    rows = grad.astype(bf16).reshape(H, HD, D)
    for h in range(H):
        r = order[H + h]
        out[r, 0:64] = rows[h]
        index = lax.broadcasted_iota(jnp.int32, (16, D), 0)
        tail = jnp.where(index == 0, router_grad[2 * h : 2 * h + 1], 0.0)
        tail = jnp.where(index == 1, router_grad[2 * h + 1 : 2 * h + 2], tail)
        if h == 0:
            tail = jnp.where(index == 2, second[...], tail)
        out[r, 64:80] = tail.astype(bf16)


def attend_back_body(odd, datt, qkv, att, totals, cosine, sine, n1, out, weight_grad, pair, dq, dk, dv, dmix, low):
    for s in range(16):
        dmix[:, 128 * s : 128 * s + 128] = datt[s]
    rows = lax.broadcasted_iota(jnp.int32, (256, 256), 0)
    cols = lax.broadcasted_iota(jnp.int32, (256, 256), 1)
    visible = rows <= cols
    dk[...] = jnp.zeros_like(dk)
    dv[...] = jnp.zeros_like(dv)
    for i in range(8):
        here = slice(256 * i, 256 * i + 256)
        query = qkv[0:64, here]
        inverse = 1.0 / totals[:, here]
        grad_att = dmix[:, here].astype(f32)
        delta = jnp.sum(grad_att * att[:, here], 0, keepdims=True) * inverse
        grad_mix = (grad_att * inverse).astype(bf16)
        for at, diagonal in ((slice(0, 256 * i), False), (here, True)):
            if at.stop == 0:
                continue
            key = qkv[64:128, at]
            weights = jnp.exp(dot_tn(key, query) * score_scale)
            if diagonal:
                weights = jnp.where(visible, weights, 0.0)
            grad_weights = dot_tn(qkv[128:192, at], grad_mix)
            grad_scores = (weights * (grad_weights - delta)).astype(bf16)
            more = dot(key, grad_scores)
            dq[:, here] = more if not diagonal or i == 0 else dq[:, here] + more
            dk[:, at] += dot_nt(query, grad_scores)
            dv[:, at] += dot_nt(grad_mix, weights.astype(bf16))

    def unrotated(value):
        value = value * score_scale
        a, b = value[: HD // 2], value[HD // 2 :]
        cos, sin = cosine[...], sine[...]
        return jnp.concatenate([a * cos + b * sin, b * cos - a * sin], 0).astype(bf16)

    low[0:64] = unrotated(dq[...])
    low[64:128] = unrotated(dk[...])
    low[128:192] = dv[...].astype(bf16)
    for s in range(16):
        out[s] = low[:, 128 * s : 128 * s + 128]
    grads = dot(low[...], n1[...].reshape(SEQ, D))
    weight_grad[...] = grads
    pair[...] = jnp.where(odd[0] == 1, grads[64:128], grads[128:192]).astype(bf16)


def hidden_grad_body(recv, hid, gain, grad_mid, wq, wk, wv, out):
    got = recv[...]
    grad_q = got[:, 0:64].reshape(D, TOK).T
    pairs = got[:, 64:192].astype(f32).reshape(KV, 2, 128, TOK)
    pairs = (pairs[:, 0] + pairs[:, 1]).astype(bf16)
    grad_k = pairs[:, 0:64].reshape(KV * HD, TOK).T
    grad_v = pairs[:, 64:128].reshape(KV * HD, TOK).T
    grad = dot_nt(grad_q, wq[...]) + dot_nt(grad_k, wk[...]) + dot_nt(grad_v, wv[...])
    hidden = hid[...].astype(f32)
    r1 = lax.rsqrt(jnp.mean(hidden * hidden, -1, keepdims=True) + epsilon)
    g1 = grad * gain[...]
    back = r1 * g1 - hidden * r1 * r1 * r1 * jnp.mean(g1 * hidden, -1, keepdims=True)
    out[...] = (grad_mid[...] + back).astype(bf16)


def slices_body(order, odd, weight_grad, pair, o0, o1, o2, o3, out):
    own = jnp.where(odd[0] == 1, weight_grad[128:192], weight_grad[64:128]) + pair[...].astype(f32)
    rest = added([o0[...], o1[...], o2[...], o3[...]])
    for b in range(8):
        here = slice(128 * b, 128 * b + 128)
        r = order[b]
        out[r, 0:64] = weight_grad[0:64, here].astype(bf16)
        out[r, 64:128] = own[:, here].astype(bf16)
        out[r, 128:208] = rest[:, here].astype(bf16)


def assemble_body(
    table, *refs
):
    mine, theirs = refs[0:4], refs[4:8]
    wq, wk, wv, gain = refs[8:12]
    q_out, k_out, v_out, o_out, r_out, f_out, s_out = refs[12:19]
    tiles, tails = refs[19:21]
    g = pl.program_id(0)

    def place(parts, base):
        for i in range(4):
            for j in range(4):
                h = table[8 + base + 4 * i + j]
                block = parts[i][j, 0]
                tiles[h] = block[0:128].astype(f32)
                o_out[pl.ds(pl.multiple_of(h * 64, 64), 64)] = block[128:192].astype(f32)
                tails[h] = block[192:208].astype(f32)

    @pl.when(g < 4)
    def _():
        place(mine, 0)

    @pl.when(g >= 4)
    def _():
        place(theirs, 16)

    for p in range(8):
        q_out[:, 128 * p : 128 * p + 128] = jnp.concatenate([tiles[2 * p][:, :64], tiles[2 * p + 1][:, :64]], 1)
    for m in range(4):
        here = slice(128 * m, 128 * m + 128)
        k_out[:, here] = jnp.concatenate([tiles[4 * m][:, 64:], tiles[4 * m + 2][:, 64:]], 1)
        v_out[:, here] = jnp.concatenate([tiles[4 * m + 1][:, 64:], tiles[4 * m + 3][:, 64:]], 1)
    for h in range(16):
        r_out[2 * h : 2 * h + 2] = tails[h][0:2]
    s_out[...] = jnp.broadcast_to(tails[0][2:3], s_out.shape)
    total = jnp.sum(q_out[...] * wq[...].astype(f32), 1, keepdims=True)
    total = total + jnp.sum(k_out[...] * wk[...].astype(f32), 1, keepdims=True)
    total = total + jnp.sum(v_out[...] * wv[...].astype(f32), 1, keepdims=True)
    f_out[...] = total / gain[...]


def assemble(table, mine, theirs, wq, wk, wv, gain):
    rows = 208
    grid_spec = pltpu.PrefetchScalarGridSpec(
        num_scalar_prefetch=1,
        grid=(8,),
        in_specs=[pl.BlockSpec((4, 1, rows, 128), lambda g, t: (0, g % 4, 0, 0))] * 8
        + [
            pl.BlockSpec((128, 1024), lambda g, t: (t[g], 0)),
            pl.BlockSpec((128, 512), lambda g, t: (t[g], 0)),
            pl.BlockSpec((128, 512), lambda g, t: (t[g], 0)),
            pl.BlockSpec((128, 1), lambda g, t: (t[g], 0)),
        ],
        out_specs=[
            pl.BlockSpec((128, 1024), lambda g, t: (t[g], 0)),
            pl.BlockSpec((128, 512), lambda g, t: (t[g], 0)),
            pl.BlockSpec((128, 512), lambda g, t: (t[g], 0)),
            pl.BlockSpec((1024, 128), lambda g, t: (0, t[g])),
            pl.BlockSpec((32, 128), lambda g, t: (0, t[g])),
            pl.BlockSpec((128, 1), lambda g, t: (t[g], 0)),
            pl.BlockSpec((8, 128), lambda g, t: (0, t[g])),
        ],
        scratch_shapes=[pltpu.VMEM((16, 128, 128), f32), pltpu.VMEM((16, 16, 128), f32)],
    )
    return pl.pallas_call(
        assemble_body,
        grid_spec=grid_spec,
        out_shape=[
            shape((1024, 1024), f32),
            shape((1024, 512), f32),
            shape((1024, 512), f32),
            shape((1024, 1024), f32),
            shape((32, 1024), f32),
            shape((1024, 1), f32),
            shape((8, 1024), f32),
        ],
        compiler_params=pltpu.CompilerParams(vmem_limit_bytes=48 * 1024 * 1024),
        name="assemble",
    )(table, *mine, *theirs, wq, wk, wv, gain)


def slot_codes(routes):
    chosen = (routes.T[:, None, :] == jnp.arange(EXPERTS)[None, :, None]).any(0)
    before = jnp.triu(jnp.ones((TOK, TOK), f32), 1)
    rank = jnp.dot(chosen.astype(bf16), before.astype(bf16), preferred_element_type=f32)
    kept = chosen & (rank < CAPACITY)
    return jnp.where(kept, rank, jnp.where(chosen, -1.0, -2.0))


def on_device(
    hidden_in,
    routes,
    first_gain,
    query_weight,
    key_weight,
    value_weight,
    output_weight,
    second_gain,
    router_weight,
    gateup_weight,
    down_weight,
    cotangent,
):
    dp, me = lax.axis_index("dp"), lax.axis_index("expert")
    z, core = dp // 2, dp % 2
    x, y = me // 4, me % 4
    steps = jnp.arange(4)

    def places(which):
        zero = ((x + steps[:, None]) % 4) * 4 + (y + steps[None, :]) % 4
        one = ((x + steps[None, :]) % 4) * 4 + (y + steps[:, None]) % 4
        return jnp.where(which == 0, zero, one).astype(jnp.int32)

    sources = places(core)
    vm = pl.BlockSpec(memory_space=pltpu.VMEM)
    sm = pl.BlockSpec(memory_space=pltpu.SMEM)
    anyspace = pl.BlockSpec(memory_space=pl.ANY)

    gain_one = first_gain.astype(f32)[None]
    gain_two = second_gain.astype(f32)[None]
    router_t = router_weight.T

    codes = slot_codes(routes)
    packed = jnp.pad(codes.astype(bf16).reshape(4, D), ((0, 12), (0, 0)))
    cot_all = lax.all_gather(jnp.concatenate([cotangent, packed], 0), "expert", axis=0, tiled=False)
    code_all = cot_all[:, TOK : TOK + 4].reshape(16, EXPERTS, TOK).astype(f32)
    code_mine = jnp.roll(code_all, -2 * me, axis=1)
    router_mine = jnp.roll(router_t, -2 * me, axis=0)

    inverse = 10000.0 ** (-jnp.arange(0, HD, 2).astype(f32) / HD)
    all_angles = inverse[:, None] * jnp.arange(SEQ).astype(f32)[None, :]
    cos_all, sin_all = jnp.cos(all_angles), jnp.sin(all_angles)
    angles = inverse[:, None] * (me * TOK + jnp.arange(TOK)).astype(f32)[None, :]

    to_heads, normed_one = call(
        project_body,
        [shape((16, 192, TOK)), shape((TOK, D))],
        [hidden_in, gain_one, query_weight, key_weight, value_weight, jnp.cos(angles), jnp.sin(angles)],
        flops=2 * TOK * D * 2048,
        moved=5 << 20,
        name="project",
    )
    at_heads = lax.all_to_all(to_heads, "expert", split_axis=0, concat_axis=0, tiled=True)
    normed_all = lax.all_gather(normed_one, "expert", axis=0, tiled=False)
    att_send, att, totals, qkv = call(
        attend_body,
        [shape((16, HD, TOK)), shape((HD, SEQ), f32), shape((1, SEQ), f32), shape((192, SEQ))],
        [at_heads],
        flops=4 * 10**9,
        moved=3 << 20,
        name="attend",
    )
    att_t = lax.all_to_all(att_send, "expert", split_axis=0, concat_axis=0, tiled=True)
    middle, scale_two, normed_two = call(
        middle_body,
        [shape((TOK, D), f32), shape((TOK, 128), f32), shape((TOK, D))],
        [att_t, hidden_in, output_weight, gain_two],
        flops=2 * TOK * D * D,
        moved=4 << 20,
        name="middle",
    )

    row = jnp.stack(gather_axis(normed_two, along_u))
    chunks = gather_axis(row, along_v)
    worked = {}
    for i in (0, 1, 3, 2):
        ids = jnp.concatenate([sources[i], me[None].astype(jnp.int32)])
        worked[i] = call(
            expert_body,
            [
                shape((4, TOK + 16, D)),
                shape((2, 256, D)),
                shape((2, 256, D)),
                shape((2, 256, FF)),
                shape((2, 256, 2 * FF)),
            ],
            [ids, chunks[i], cot_all, code_mine, router_mine, gateup_weight, down_weight],
            scratch=[
                pltpu.VMEM((4, TOK, D), bf16),
                pltpu.VMEM((2, D, 2 * FF), bf16),
                pltpu.VMEM((2, FF, D), bf16),
                pltpu.VMEM((4, TOK, D), bf16),
                pltpu.SemaphoreType.DMA((8,)),
            ],
            specs=[sm, vm, anyspace, vm, vm, anyspace, anyspace],
            flops=4 * 10**9,
            moved=14 << 20,
            name="experts",
        )
    parts = sum_axis([worked[i][0] for i in range(4)], along_v)
    grad_rows = sum_axis([added([p[j] for p in parts]).astype(bf16) for j in range(4)], along_u)

    saved = [[worked[i][k] for i in range(4)] for k in range(1, 5)]

    def half(width):
        return pl.BlockSpec((1, 256, width), lambda e: (e, 0, 0))

    gateup_grad, down_grad = pl.pallas_call(
        expert_grad_body,
        grid=(2,),
        in_specs=[half(D)] * 8 + [half(FF)] * 4 + [half(2 * FF)] * 4,
        out_specs=[pl.BlockSpec((1, D, 2 * FF), lambda e: (e, 0, 0)), pl.BlockSpec((1, FF, D), lambda e: (e, 0, 0))],
        out_shape=[shape((2, D, 2 * FF)), shape((2, FF, D))],
        scratch_shapes=[
            pltpu.VMEM((1024, D), bf16),
            pltpu.VMEM((1024, D), bf16),
            pltpu.VMEM((1024, FF), bf16),
            pltpu.VMEM((1024, 2 * FF), bf16),
        ],
        compiler_params=pltpu.CompilerParams(vmem_limit_bytes=56 * 1024 * 1024),
        cost_estimate=pl.CostEstimate(flops=7 * 10**9, bytes_accessed=24 << 20, transcendentals=0),
        name="expert_grads",
    )(*saved[0], *saved[1], *saved[2], *saved[3])
    gateup_grad, down_grad = lax.psum((gateup_grad, down_grad), "dp")

    results = []
    for i in range(4):
        (result,) = call(
            expert_result_body,
            [shape((4, TOK, D))],
            [sources[i], saved[2][i], code_mine, down_weight],
            scratch=[pltpu.VMEM((4, TOK, D), bf16)],
            specs=[sm, vm, vm, vm],
            flops=10**9,
            moved=4 << 20,
            name="expert_results",
        )
        results.append(result)
    result_parts = sum_axis(results, along_v)
    result_rows = sum_axis([added([p[j] for p in result_parts]).astype(bf16) for j in range(4)], along_u)
    layer_out = (middle + added(result_rows)).astype(bf16)

    grad_middle, grad_middle_low, to_back, router_grad, second_part = call(
        norm_back_body,
        [
            shape((TOK, D), f32),
            shape((TOK, D)),
            shape((H, HD, TOK)),
            shape((EXPERTS, D), f32),
            shape((1, D), f32),
        ],
        [
            *grad_rows,
            normed_two,
            middle,
            scale_two,
            gain_two,
            cotangent,
            codes,
            router_t,
            output_weight,
        ],
        flops=3 * 10**8,
        moved=5 << 20,
        name="norm_back",
    )
    at_back = lax.all_to_all(to_back, "expert", split_axis=0, concat_axis=0, tiled=True)

    order = sources.reshape(-1)
    rank_of = jnp.sum(jnp.where(order[None, :] == jnp.arange(16)[:, None], jnp.arange(16)[None, :], 0), 1)
    (o_part,) = call(
        output_grad_body,
        [shape((16, 80, D))],
        [jnp.concatenate([order, rank_of]).astype(jnp.int32), att_t, grad_middle_low, router_grad, second_part],
        specs=[sm, vm, vm, vm, vm],
        flops=2 * TOK * D * D,
        moved=5 << 20,
        name="output_grad",
    )
    o_rows = sum_axis([o_part[4 * i : 4 * i + 4] for i in range(4)], along_v)
    o_rows = sum_axis([added([p[j] for p in o_rows]).astype(bf16) for j in range(4)], along_u)

    odd = (me % 2)[None].astype(jnp.int32)
    to_tokens, weight_grad, pair = call(
        attend_back_body,
        [shape((16, 192, TOK)), shape((192, D), f32), shape((HD, D))],
        [odd, at_back, qkv, att, totals, cos_all, sin_all, normed_all],
        scratch=[
            pltpu.VMEM((HD, SEQ), f32),
            pltpu.VMEM((HD, SEQ), f32),
            pltpu.VMEM((HD, SEQ), f32),
            pltpu.VMEM((HD, SEQ), bf16),
            pltpu.VMEM((192, SEQ), bf16),
        ],
        specs=[sm] + [vm] * 7,
        flops=10**10,
        moved=10 << 20,
        name="attend_back",
    )
    at_tokens = lax.all_to_all(to_tokens, "expert", split_axis=0, concat_axis=0, tiled=True)
    (hidden_grad,) = call(
        hidden_grad_body,
        [shape((TOK, D))],
        [at_tokens, hidden_in, gain_one, grad_middle, query_weight, key_weight, value_weight],
        flops=2 * TOK * D * 2048,
        moved=6 << 20,
        name="hidden_grad",
    )

    pair = send(pair, pair_head())
    blocks = jnp.arange(8)
    offsets = ((blocks // 4 + core) % 2) * 4 + ((blocks % 4) - z) % 4
    (slices,) = call(
        slices_body,
        [shape((8, 208, 128))],
        [offsets.astype(jnp.int32), odd, weight_grad, pair, *o_rows],
        specs=[sm, sm] + [vm] * 6,
        flops=10**6,
        moved=3 << 20,
        name="slices",
    )
    halves = added([slices[:4], send(slices[4:], other_core())]).astype(bf16)
    block = added(sum_axis([halves[k] for k in range(4)], along_z))
    block = jnp.concatenate([block[:128].T, block[128:]], 0).astype(bf16)
    block = jnp.stack(gather_axis(block, along_z))
    block = jnp.stack(gather_axis(block, along_u))
    mine = gather_axis(block, along_v)
    theirs = [send(part, other_core()) for part in mine]
    own_blocks = jnp.concatenate([core * 4 + (z + steps) % 4, (1 - core) * 4 + (z + steps) % 4])
    table = jnp.concatenate([own_blocks, places(core).reshape(-1), places(1 - core).reshape(-1)]).astype(jnp.int32)
    query_grad, key_grad, value_grad, output_grad, router_out, first_grad, second_grad = assemble(
        table, mine, theirs, query_weight, key_weight, value_weight, first_gain.astype(f32)[:, None]
    )
    return (
        layer_out,
        hidden_grad,
        gateup_grad.astype(f32),
        down_grad.astype(f32),
        query_grad,
        key_grad,
        value_grad,
        output_grad,
        router_out.T,
        first_grad[:, 0],
        second_grad[0],
    )


def solution(mesh):
    rows = P(("dp", "expert"), None)
    experts = P("expert", None, None)
    return jax.shard_map(
        on_device,
        mesh=mesh,
        in_specs=(rows, rows, P(), P(), P(), P(), P(), P(), P(), experts, experts, rows),
        out_specs=(rows, rows, experts, experts, P(), P(), P(), P(), P(), P(), P()),
        check_vma=False,
    )
```

time: 802 us -> 390 us (0.49)
  waiting for transfers between devices: 352 us -> 82.6 us
  blocking collectives: 131 us -> 24.5 us
  Pallas kernels: 0 us -> 93 us
  local copies, waits for them, and re-layouts: 129 us -> 41.4 us
  matrix products: 73.4 us -> 0.74 us
  starting transfers between devices: 20.6 us -> 84.7 us
  other arithmetic: 70.4 us -> 40.7 us
    all_to_all x3, waiting for transfers between devices: 123 us -> 9.94 us  [the longest x1 9.94 us: on_device(): lax.all_to_all(att_send, 'expert', split_axis=0, concat_axis=0, tiled=True)]
    psum x2 -> x1, waiting for transfers between devices: 93.8 us -> 0.01 us  [on_device(): gateup_grad, down_grad = lax.psum((gateup_grad, down_grad), 'dp')]
    unnamed x5 -> x3, waiting for transfers between devices: 93.6 us -> 0.05 us
    pallas_call x0 -> x18, Pallas kernels: none -> 93 us  [the longest x16 67.7 us: call(): pl.pallas_call(body, out_shape=outs, in_specs=[vmem] * len(args) if specs...]
    dot_general x28 -> x1, matrix products: 73.4 us -> 0.74 us  [slot_codes(): jnp.dot(chosen.astype(bf16), before.astype(bf16), preferred_element_type=...]
    ppermute x0 -> x42, waiting for transfers between devices: none -> 72.6 us  [send(): return lax.ppermute(array, AXES, pairs)]
    ppermute x0 -> x42, starting transfers between devices: none -> 71.7 us  [send(): return lax.ppermute(array, AXES, pairs)]
    psum x1 -> x0, blocking collectives: 66.8 us -> none  [on_device(): lax.psum((first_grad, query_grad, key_grad, value_grad, output_grad, rout...]
  transfers between devices with their start and end apart: 7 -> 48, of which waited for: 7 -> 18; matrix products, arithmetic and copies ran while one was open for 15% -> 12% of each run, Pallas kernels for 0% -> 21%
where the time goes in v1:
time: 390 us; the launch traced here: 383 us
  Pallas kernels  93 us (24%)
  starting transfers between devices  84.7 us (22%)
  waiting for transfers between devices  82.6 us (21%)
  local copies, waits for them, and re-layouts  41.4 us (11%)
  other arithmetic  40.7 us (10%)
  blocking collectives  24.5 us (6%)
  between operations  14.9 us (4%)
    ppermute x42, waiting for transfers between devices, send(): return lax.ppermute(array, AXES, pairs)  72.6 us
    ppermute x42, starting transfers between devices, send(): return lax.ppermute(array, AXES, pairs)  71.7 us
    pallas_call x16, Pallas kernels, call(): pl.pallas_call(body, out_shape=outs, in_specs=[vmem] * len(args) if specs...  67.7 us
    unnamed x152, local copies, waits for them, and re-layouts  32.9 us
    all_to_all x1, blocking collectives, on_device(): lax.all_to_all(to_heads, 'expert', split_axis=0, concat_axis=0, tiled=True)  24.5 us
    pallas_call x1, Pallas kernels, assemble(): pl.pallas_call(assemble_body, grid_spec=grid_spec, out_shape=[shape((1024...  14.3 us
    pallas_call x1, Pallas kernels, on_device(): pl.pallas_call(expert_grad_body, grid=(2,), in_specs=[half(D)] * 8 + [hal...  11.1 us
    all_to_all x1, waiting for transfers between devices, on_device(): lax.all_to_all(att_send, 'expert', split_axis=0, concat_axis=0, tiled=True)  9.94 us
  transfers between devices with their start and end apart: 48, of which 18 were waited for; matrix products, arithmetic and copies ran while one was open for 12% of the time, Pallas kernels for 21%

profile of v1, /device:TPU:1, one launch (start us, length us, event | category | flops | bytes accessed | tf_op | source)
XLA Modules:
  0.0 382.7 jit_solution(9793650485847978313)
XLA Ops:
  17.6 24.5 %all_to_all.20.recv = bf16[16,192,128]{2,1,0:T(8,128)(2,1)S(1)} all-to-all(bf16[16,192,128]{2,1,0:T(8,128)(2,1)S(1)} %get-tuple-element.57), channel_id=1, replica_groups=mesh['dp'=8,'expert'=16] {'expert'}, dimensions={0} | all-to-all | bytes 1572864 | tf_op jit(solution)/shard_map/all_to_all | solution.py:524
  42.2 4.1 %attend.1 = (bf16[16,64,128]{2,1,0:T(8,128)(2,1)}, f32[64,2048]{1,0:T(8,128)S(1)}, f32[1,2048]{1,0:T(1,128)S(1)}, bf16[192,2048]{1,0:T(8,128)(2,1)S(1)}) custom-call(bf16[16,192,128]{2,1,0:T(8,128)(2,1)S(1)} %all_to_all.20.recv), custom_call_target="tpu_custom_call" | custom-call | flops 4000000000 | bytes 3145728 | tf_op jit(solution)/shard_map/attend/pallas_call | solution.py:97
  48.1 4.0 %all-to-all-start.1 = ((bf16[16,64,128]{2,1,0:T(8,128)(2,1)}), bf16[16,64,128]{2,1,0:T(8,128)(2,1)S(1)}, u32[]{:S(2)}, u32[]{:S(2)}) async-start(bf16[16,64,128]{2,1,0:T(8,128)(2,1)} %get-tuple-element.58), calls=%async_computation.1 | async-start | bytes 524288 | tf_op jit(solution)/shard_map/all_to_all | solution.py:534
  52.1 9.9 %all-to-all-done.1.att_t.att = bf16[16,64,128]{2,1,0:T(8,128)(2,1)S(1)} async-done(((bf16[16,64,128]{2,1,0:T(8,128)(2,1)}), bf16[16,64,128]{2,1,0:T(8,128)(2,1)S(1)}, u32[]{:S(2)}, u32[]{:S(2)}) %all-to-all-start.1) | async-done | bytes 262176 | tf_op jit(solution)/shard_map/all_to_all | solution.py:534
  66.5 8.8 %collective-permute-done.2 = bf16[128,1024]{1,0:T(8,128)(2,1)} collective-permute-done((bf16[128,1024]{1,0:T(8,128)(2,1)S(1)}, bf16[128,1024]{1,0:T(8,128)(2,1)}, u32[]{:S(2)}, u32[]{:S(2)}) %collective-permute-start.2) | collective-permute-done | bytes 262176 | tf_op jit(solution)/shard_map/ppermute | solution.py:77
  75.2 6.1 %collective-permute-done.1 = bf16[128,1024]{1,0:T(8,128)(2,1)} collective-permute-done((bf16[128,1024]{1,0:T(8,128)(2,1)S(1)}, bf16[128,1024]{1,0:T(8,128)(2,1)}, u32[]{:S(2)}, u32[]{:S(2)}) %collective-permute-start.1) | collective-permute-done | bytes 262176 | tf_op jit(solution)/shard_map/ppermute | solution.py:77
  101.9 8.9 %experts.7 = (bf16[4,144,1024]{2,1,0:T(8,128)(2,1)}, bf16[2,256,1024]{2,1,0:T(8,128)(2,1)S(1)}, bf16[2,256,1024]{2,1,0:T(8,128)(2,1)S(1)}, bf16[2,256,512]{2,1,0:T(8,128)(2,1)S(1)}, bf16[2,256,1024]{2,1,0:T(8,128)(2,1)S(1)}) custom-call(s32[5]{0:T(128)S(1)} %copy-done.47, bf16[4,128,1024]{2,1,0:T(8,128)(2,1)} %collective-permute-done.7.n2, ...), custom_call_target="tpu_custom_call" | custom-call | flops 4000000000 | bytes 14680064 | tf_op jit(solution)/shard_map/experts/pallas_call | solution.py:97
  115.6 8.9 %experts.6 = (bf16[4,144,1024]{2,1,0:T(8,128)(2,1)}, bf16[2,256,1024]{2,1,0:T(8,128)(2,1)S(1)}, bf16[2,256,1024]{2,1,0:T(8,128)(2,1)S(1)}, bf16[2,256,512]{2,1,0:T(8,128)(2,1)S(1)}, bf16[2,256,1024]{2,1,0:T(8,128)(2,1)S(1)}) custom-call(s32[5]{0:T(128)S(1)} %copy-done.46, bf16[4,128,1024]{2,1,0:T(8,128)(2,1)} %collective-permute-done.5.n2, ...), custom_call_target="tpu_custom_call" | custom-call | flops 4000000000 | bytes 14680064 | tf_op jit(solution)/shard_map/experts/pallas_call | solution.py:97
  129.2 8.9 %experts.5 = (bf16[4,144,1024]{2,1,0:T(8,128)(2,1)}, bf16[2,256,1024]{2,1,0:T(8,128)(2,1)S(1)}, bf16[2,256,1024]{2,1,0:T(8,128)(2,1)S(1)}, bf16[2,256,512]{2,1,0:T(8,128)(2,1)S(1)}, bf16[2,256,1024]{2,1,0:T(8,128)(2,1)S(1)}) custom-call(s32[5]{0:T(128)S(1)} %copy-done.45, bf16[4,128,1024]{2,1,0:T(8,128)(2,1)} %collective-permute-done.3.n2, ...), custom_call_target="tpu_custom_call" | custom-call | flops 4000000000 | bytes 14680064 | tf_op jit(solution)/shard_map/experts/pallas_call | solution.py:97
  147.3 8.9 %experts.4 = (bf16[4,144,1024]{2,1,0:T(8,128)(2,1)}, bf16[2,256,1024]{2,1,0:T(8,128)(2,1)S(1)}, bf16[2,256,1024]{2,1,0:T(8,128)(2,1)S(1)}, bf16[2,256,512]{2,1,0:T(8,128)(2,1)S(1)}, bf16[2,256,1024]{2,1,0:T(8,128)(2,1)S(1)}) custom-call(s32[5]{0:T(128)S(1)} %pad_add_fusion.src, bf16[4,128,1024]{2,1,0:T(8,128)(2,1)} %pad_maximum_fusion.n2, ...), custom_call_target="tpu_custom_call" | custom-call | flops 4000000000 | bytes 14680064 | tf_op jit(solution)/shard_map/experts/pallas_call | solution.py:97
  157.2 10.9 %collective-permute-done.12 = bf16[4,144,1024]{2,1,0:T(8,128)(2,1)} collective-permute-done((bf16[4,144,1024]{2,1,0:T(8,128)(2,1)}, bf16[4,144,1024]{2,1,0:T(8,128)(2,1)}, u32[]{:S(2)}, u32[]{:S(2)}) %collective-permute-start.12) | collective-permute-done | bytes 1179680 | tf_op jit(solution)/shard_map/ppermute | solution.py:77
  178.8 3.8 collective-permute-done.16.p2
  187.0 4.3 %all-to-all-start.2 = ((bf16[16,64,128]{2,1,0:T(8,128)(2,1)}), bf16[16,64,128]{2,1,0:T(8,128)(2,1)S(1)}, u32[]{:S(2)}, u32[]{:S(2)}) async-start(bf16[16,64,128]{2,1,0:T(8,128)(2,1)} %copy-done.31), calls=%async_computation.2 | async-start | bytes 524288 | tf_op jit(solution)/shard_map/all_to_all | solution.py:638
  201.7 10.2 %attend_back.1 = (bf16[16,192,128]{2,1,0:T(8,128)(2,1)S(1)}, f32[192,1024]{1,0:T(8,128)S(1)}, bf16[64,1024]{1,0:T(8,128)(2,1)S(1)}) custom-call(s32[1]{0:T(128)} %bitcast.18.odd, bf16[16,64,128]{2,1,0:T(8,128)(2,1)S(1)} %all-to-all-done.2.datt, bf16[192,2048]{1,0:T(8,128)(2,1)S(1)} %copy-done.61, f32[64,2048]{1,0:T(8,128)S(1)} %copy-done.63, ...), custom_call_target="tpu_custom_call" | custom-call | flops 10000000000 | bytes 10485760 | tf_op jit(solution)/shard_map/attend_back/pallas_call | solution.py:97
  233.2 5.2 %collective-permute-start.25 = (bf16[4,208,128]{2,1,0:T(8,128)(2,1)S(1)}, bf16[4,208,128]{2,1,0:T(8,128)(2,1)}, u32[]{:S(2)}, u32[]{:S(2)}) collective-permute-start(bf16[4,208,128]{2,1,0:T(8,128)(2,1)S(1)} %slice.318), channel_id=1, source_target_pairs={{0,16},{1,17},{2,18},{3,19},{4,20},{5,21},{6,22},{7,23},{8,24},{9,... | collective-permute-start | bytes 638984 | tf_op jit(solution)/shard_map/ppermute | solution.py:77
  238.4 11.1 %expert_grads.1 = (bf16[2,1024,1024]{2,1,0:T(8,128)(2,1)}, bf16[2,512,1024]{2,1,0:T(8,128)(2,1)}) custom-call(bf16[2,256,1024]{2,1,0:T(8,128)(2,1)} %copy-done.57, bf16[2,256,1024]{2,1,0:T(8,128)(2,1)} %copy-done.54, bf16[2,256,1024]{2,1,0:T(8,128)(2,1)} %copy-done.51, bf16[2,256,1024]{2,1,0:T(8,128)(2,1)} %copy-done.48, bf16[2,256,1024]{2,1,0:T(8,128)(2,1)} %copy-done.58, ...), custom_call_target="tpu_custom_call" | custom-call | flops 7000000000 | bytes 25165824 | tf_op jit(solution)/shard_map/expert_grads/pallas_call | solution.py:579
  285.4 3.7 collective-permute-start.36
  296.6 7.2 %collective-permute-done.11 = bf16[128,1024]{1,0:T(8,128)(2,1)S(1)} collective-permute-done((bf16[128,1024]{1,0:T(8,128)(2,1)S(1)}, bf16[128,1024]{1,0:T(8,128)(2,1)S(1)}, u32[]{:S(2)}, u32[]{:S(2)}) %collective-permute-start.11) | collective-permute-done | bytes 262176 | tf_op jit(solution)/shard_map/ppermute | solution.py:77
  303.8 4.8 %collective-permute-start.38 = (bf16[4,4,208,128]{3,2,1,0:T(8,128)(2,1)}, bf16[4,4,208,128]{3,2,1,0:T(8,128)(2,1)}, u32[]{:S(2)}, u32[]{:S(2)}) collective-permute-start(bf16[4,4,208,128]{3,2,1,0:T(8,128)(2,1)} %pad_maximum_fusion.1.refs_0_), channel_id=1, source_target_pairs={{0,16},{1,17},{2,18},{3,19},{4,20},{5,21},{6,22},{7,23},{8,24},{9,... | collective-permute-start | bytes 2555912 | tf_op jit(solution)/shard_map/ppermute | solution.py:77
  308.6 12.8 %collective-permute-start.39 = (bf16[4,4,208,128]{3,2,1,0:T(8,128)(2,1)}, bf16[4,4,208,128]{3,2,1,0:T(8,128)(2,1)}, u32[]{:S(2)}, u32[]{:S(2)}) collective-permute-start(bf16[4,4,208,128]{3,2,1,0:T(8,128)(2,1)} %collective-permute-done.35.refs_1_), channel_id=1, source_target_pairs={{0,16},{1,17},{2,18},{3,19},{4,20},{5,21},{6,22},{7,23},{8,24},{9,... | collective-permute-start | bytes 2555912 | tf_op jit(solution)/shard_map/ppermute | solution.py:77
  322.5 4.6 %all-to-all-start.3 = ((bf16[16,192,128]{2,1,0:T(8,128)(2,1)}), bf16[16,192,128]{2,1,0:T(8,128)(2,1)}, u32[]{:S(2)}, u32[]{:S(2)}) async-start(bf16[16,192,128]{2,1,0:T(8,128)(2,1)} %copy-done.17), calls=%async_computation.3 | async-start | bytes 1572864 | tf_op jit(solution)/shard_map/all_to_all | solution.py:671
  329.6 12.8 %collective-permute-done.9 = bf16[128,1024]{1,0:T(8,128)(2,1)} collective-permute-done((bf16[128,1024]{1,0:T(8,128)(2,1)}, bf16[128,1024]{1,0:T(8,128)(2,1)}, u32[]{:S(2)}, u32[]{:S(2)}) %collective-permute-start.9) | collective-permute-done | bytes 262176 | tf_op jit(solution)/shard_map/ppermute | solution.py:77
  350.7 6.8 %convert_element_type.346 = f32[2,1024,1024]{2,1,0:T(8,128)} convert(bf16[2,1024,1024]{2,1,0:T(8,128)(2,1)} %get-tuple-element.103) | non-fusion elementwise | flops 2097152 | bytes 12582912 | tf_op jit(solution)/shard_map/convert_element_type | solution.py:708
  360.0 14.3 %assemble.1 = (f32[1024,1024]{1,0:T(8,128)}, f32[1024,512]{1,0:T(8,128)}, f32[1024,512]{1,0:T(8,128)}, f32[1024,1024]{1,0:T(8,128)}, f32[32,1024]{1,0:T(8,128)},...) custom-call(s32[40]{0:T(128)S(1)} %pad_add_fusion.4.table, bf16[4,4,208,128]{3,2,1,0:T(8,128)(2,1)} %pad_maximum_fusion.1.refs_0_, ...), custom_call_target="tpu_custom_call" | custom-call | tf_op jit(solution)/shard_map/assemble/pallas_call | solution.py:446
  (301 shorter events, 162.1 us)
Async XLA Ops:
  7.2 85.9 %all-gather.5.cloned.1.call-start = ((), (), s32[]{:S(2)}) async-start(), calls=%async_computation.4 | async-start | bytes 5013504 | tf_op jit(solution)/shard_map/all_gather | solution.py:506
  10.4 191.3 %all-gather.7.cloned.1.call-start = ((), (), s32[]{:S(2)}) async-start(), calls=%async_computation.5 | async-start | bytes 4456448 | tf_op jit(solution)/shard_map/all_gather | solution.py:525
  63.0 18.4 %collective-permute-start.1 = (bf16[128,1024]{1,0:T(8,128)(2,1)S(1)}, bf16[128,1024]{1,0:T(8,128)(2,1)}, u32[]{:S(2)}, u32[]{:S(2)}) collective-permute-start(bf16[128,1024]{1,0:T(8,128)(2,1)S(1)} %get-tuple-element.60.n2), channel_id=1, source_target_pairs={{0,2},{1,3},{2,0},{3,1},{4,6},{5,7},{6,4},{7,5},{8,10},{9,11},{10,... | collective-permute-start | bytes 786440 | tf_op jit(solution)/shard_map/ppermute | solution.py:77
  85.1 30.4 %collective-permute-start.5 = (bf16[4,128,1024]{2,1,0:T(8,128)(2,1)}, bf16[4,128,1024]{2,1,0:T(8,128)(2,1)}, u32[]{:S(2)}, u32[]{:S(2)}) collective-permute-start(bf16[4,128,1024]{2,1,0:T(8,128)(2,1)} %pad_maximum_fusion.n2), channel_id=1, source_target_pairs={{0,8},{1,9},{2,10},{3,11},{4,12},{5,13},{6,14},{7,15},{8,0},{9,1},... | collective-permute-start | bytes 3145736 | tf_op jit(solution)/shard_map/ppermute | solution.py:77
  90.4 38.8 %collective-permute-start.3 = (bf16[4,128,1024]{2,1,0:T(8,128)(2,1)}, bf16[4,128,1024]{2,1,0:T(8,128)(2,1)}, u32[]{:S(2)}, u32[]{:S(2)}) collective-permute-start(bf16[4,128,1024]{2,1,0:T(8,128)(2,1)} %pad_maximum_fusion.n2), channel_id=1, source_target_pairs={{0,12},{1,13},{2,14},{3,15},{4,0},{5,1},{6,2},{7,3},{8,4},{9,5},{1... | collective-permute-start | bytes 3145736 | tf_op jit(solution)/shard_map/ppermute | solution.py:77
  114.7 42.5 %collective-permute-start.14 = (bf16[4,144,1024]{2,1,0:T(8,128)(2,1)}, bf16[4,144,1024]{2,1,0:T(8,128)(2,1)}, u32[]{:S(2)}, u32[]{:S(2)}) collective-permute-start(bf16[4,144,1024]{2,1,0:T(8,128)(2,1)} %get-tuple-element.68), channel_id=1, source_target_pairs={{0,12},{1,13},{2,14},{3,15},{4,0},{5,1},{6,2},{7,3},{8,4},{9,5},{1... | collective-permute-start | bytes 3538952 | tf_op jit(solution)/shard_map/ppermute | solution.py:77
  128.3 28.9 %collective-permute-start.13 = (bf16[4,144,1024]{2,1,0:T(8,128)(2,1)}, bf16[4,144,1024]{2,1,0:T(8,128)(2,1)}, u32[]{:S(2)}, u32[]{:S(2)}) collective-permute-start(bf16[4,144,1024]{2,1,0:T(8,128)(2,1)} %get-tuple-element.67), channel_id=1, source_target_pairs={{0,8},{1,9},{2,10},{3,11},{4,12},{5,13},{6,14},{7,15},{8,0},{9,1},... | collective-permute-start | bytes 3538952 | tf_op jit(solution)/shard_map/ppermute | solution.py:77
  141.9 26.3 %collective-permute-start.12 = (bf16[4,144,1024]{2,1,0:T(8,128)(2,1)}, bf16[4,144,1024]{2,1,0:T(8,128)(2,1)}, u32[]{:S(2)}, u32[]{:S(2)}) collective-permute-start(bf16[4,144,1024]{2,1,0:T(8,128)(2,1)} %get-tuple-element.66), channel_id=1, source_target_pairs={{0,4},{1,5},{2,6},{3,7},{4,8},{5,9},{6,10},{7,11},{8,12},{9,13},{1... | collective-permute-start | bytes 3538952 | tf_op jit(solution)/shard_map/ppermute | solution.py:77
  191.3 159.4 %all-reduce.4.cloned.1.call-start = ((), (), s32[]{:S(2)}) async-start(), calls=%async_computation.6 | async-start | bytes 12582912 | tf_op jit(solution)/shard_map/psum | solution.py:595
  197.9 17.4 %collective-permute-start.21 = (bf16[4,80,1024]{2,1,0:T(8,128)(2,1)}, bf16[4,80,1024]{2,1,0:T(8,128)(2,1)}, u32[]{:S(2)}, u32[]{:S(2)}) collective-permute-start(bf16[4,80,1024]{2,1,0:T(8,128)(2,1)} %get-tuple-element.117), channel_id=1, source_target_pairs={{0,12},{1,13},{2,14},{3,15},{4,0},{5,1},{6,2},{7,3},{8,4},{9,5},{1... | collective-permute-start | bytes 1966088 | tf_op jit(solution)/shard_map/ppermute | solution.py:77
  201.1 18.0 %collective-permute-start.19 = (bf16[4,80,1024]{2,1,0:T(8,128)(2,1)}, bf16[4,80,1024]{2,1,0:T(8,128)(2,1)}, u32[]{:S(2)}, u32[]{:S(2)}) collective-permute-start(bf16[4,80,1024]{2,1,0:T(8,128)(2,1)} %get-tuple-element.116), channel_id=1, source_target_pairs={{0,4},{1,5},{2,6},{3,7},{4,8},{5,9},{6,10},{7,11},{8,12},{9,13},{1... | collective-permute-start | bytes 1966088 | tf_op jit(solution)/shard_map/ppermute | solution.py:77
  212.9 19.0 %collective-permute-start.18 = (bf16[64,1024]{1,0:T(8,128)(2,1)S(1)}, bf16[64,1024]{1,0:T(8,128)(2,1)S(1)}, u32[]{:S(2)}, u32[]{:S(2)}) collective-permute-start(bf16[64,1024]{1,0:T(8,128)(2,1)S(1)} %get-tuple-element.92), channel_id=1, source_target_pairs={{0,1},{1,0},{2,3},{3,2},{4,5},{5,4},{6,7},{7,6},{8,9},{9,8},{10,11... | collective-permute-start | bytes 393224 | tf_op jit(solution)/shard_map/ppermute | solution.py:77
  228.7 60.5 %collective-permute-start.8 = (bf16[4,128,1024]{2,1,0:T(8,128)(2,1)}, bf16[4,128,1024]{2,1,0:T(8,128)(2,1)}, u32[]{:S(2)}, u32[]{:S(2)}) collective-permute-start(bf16[4,128,1024]{2,1,0:T(8,128)(2,1)} %expert_results.7), channel_id=1, source_target_pairs={{0,12},{1,13},{2,14},{3,15},{4,0},{5,1},{6,2},{7,3},{8,4},{9,5},{1... | collective-permute-start | bytes 3145736 | tf_op jit(solution)/shard_map/ppermute | solution.py:77
  231.9 60.0 %collective-permute-start.6 = (bf16[4,128,1024]{2,1,0:T(8,128)(2,1)}, bf16[4,128,1024]{2,1,0:T(8,128)(2,1)}, u32[]{:S(2)}, u32[]{:S(2)}) collective-permute-start(bf16[4,128,1024]{2,1,0:T(8,128)(2,1)} %expert_results.6), channel_id=1, source_target_pairs={{0,8},{1,9},{2,10},{3,11},{4,12},{5,13},{6,14},{7,15},{8,0},{9,1},... | collective-permute-start | bytes 3145736 | tf_op jit(solution)/shard_map/ppermute | solution.py:77
  257.9 34.0 %collective-permute-start.4 = (bf16[4,128,1024]{2,1,0:T(8,128)(2,1)}, bf16[4,128,1024]{2,1,0:T(8,128)(2,1)}, u32[]{:S(2)}, u32[]{:S(2)}) collective-permute-start(bf16[4,128,1024]{2,1,0:T(8,128)(2,1)} %expert_results.5), channel_id=1, source_target_pairs={{0,4},{1,5},{2,6},{3,7},{4,8},{5,9},{6,10},{7,11},{8,12},{9,13},{1... | collective-permute-start | bytes 3145736 | tf_op jit(solution)/shard_map/ppermute | solution.py:77
  283.9 24.6 %collective-permute-start.35 = (bf16[4,4,208,128]{3,2,1,0:T(8,128)(2,1)}, bf16[4,4,208,128]{3,2,1,0:T(8,128)(2,1)}, u32[]{:S(2)}, u32[]{:S(2)}) collective-permute-start(bf16[4,4,208,128]{3,2,1,0:T(8,128)(2,1)} %pad_maximum_fusion.1.refs_0_), channel_id=1, source_target_pairs={{0,12},{1,13},{2,14},{3,15},{4,0},{5,1},{6,2},{7,3},{8,4},{9,5},{1... | collective-permute-start | bytes 2555912 | tf_op jit(solution)/shard_map/ppermute | solution.py:77
  285.4 35.9 %collective-permute-start.36 = (bf16[4,4,208,128]{3,2,1,0:T(8,128)(2,1)}, bf16[4,4,208,128]{3,2,1,0:T(8,128)(2,1)}, u32[]{:S(2)}, u32[]{:S(2)}) collective-permute-start(bf16[4,4,208,128]{3,2,1,0:T(8,128)(2,1)} %pad_maximum_fusion.1.refs_0_), channel_id=1, source_target_pairs={{0,8},{1,9},{2,10},{3,11},{4,12},{5,13},{6,14},{7,15},{8,0},{9,1},... | collective-permute-start | bytes 2555912 | tf_op jit(solution)/shard_map/ppermute | solution.py:77
  289.2 32.2 %collective-permute-start.37 = (bf16[4,4,208,128]{3,2,1,0:T(8,128)(2,1)}, bf16[4,4,208,128]{3,2,1,0:T(8,128)(2,1)}, u32[]{:S(2)}, u32[]{:S(2)}) collective-permute-start(bf16[4,4,208,128]{3,2,1,0:T(8,128)(2,1)} %pad_maximum_fusion.1.refs_0_), channel_id=1, source_target_pairs={{0,4},{1,5},{2,6},{3,7},{4,8},{5,9},{6,10},{7,11},{8,12},{9,13},{1... | collective-permute-start | bytes 2555912 | tf_op jit(solution)/shard_map/ppermute | solution.py:77
  296.6 30.5 %collective-permute-start.10 = (bf16[128,1024]{1,0:T(8,128)(2,1)}, bf16[128,1024]{1,0:T(8,128)(2,1)}, u32[]{:S(2)}, u32[]{:S(2)}) collective-permute-start(bf16[128,1024]{1,0:T(8,128)(2,1)} %get-tuple-element.115), channel_id=1, source_target_pairs={{0,2},{1,3},{2,0},{3,1},{4,6},{5,7},{6,4},{7,5},{8,10},{9,11},{10,... | collective-permute-start | bytes 786440 | tf_op jit(solution)/shard_map/ppermute | solution.py:77
  303.8 56.2 %collective-permute-start.38 = (bf16[4,4,208,128]{3,2,1,0:T(8,128)(2,1)}, bf16[4,4,208,128]{3,2,1,0:T(8,128)(2,1)}, u32[]{:S(2)}, u32[]{:S(2)}) collective-permute-start(bf16[4,4,208,128]{3,2,1,0:T(8,128)(2,1)} %pad_maximum_fusion.1.refs_0_), channel_id=1, source_target_pairs={{0,16},{1,17},{2,18},{3,19},{4,20},{5,21},{6,22},{7,23},{8,24},{9,... | collective-permute-start | bytes 2555912 | tf_op jit(solution)/shard_map/ppermute | solution.py:77
  308.6 51.5 %collective-permute-start.39 = (bf16[4,4,208,128]{3,2,1,0:T(8,128)(2,1)}, bf16[4,4,208,128]{3,2,1,0:T(8,128)(2,1)}, u32[]{:S(2)}, u32[]{:S(2)}) collective-permute-start(bf16[4,4,208,128]{3,2,1,0:T(8,128)(2,1)} %collective-permute-done.35.refs_1_), channel_id=1, source_target_pairs={{0,16},{1,17},{2,18},{3,19},{4,20},{5,21},{6,22},{7,23},{8,24},{9,... | collective-permute-start | bytes 2555912 | tf_op jit(solution)/shard_map/ppermute | solution.py:77
  321.3 38.7 %collective-permute-start.40 = (bf16[4,4,208,128]{3,2,1,0:T(8,128)(2,1)}, bf16[4,4,208,128]{3,2,1,0:T(8,128)(2,1)}, u32[]{:S(2)}, u32[]{:S(2)}) collective-permute-start(bf16[4,4,208,128]{3,2,1,0:T(8,128)(2,1)} %collective-permute-done.36.refs_2_), channel_id=1, source_target_pairs={{0,16},{1,17},{2,18},{3,19},{4,20},{5,21},{6,22},{7,23},{8,24},{9,... | collective-permute-start | bytes 2555912 | tf_op jit(solution)/shard_map/ppermute | solution.py:77
  321.4 38.7 %collective-permute-start.41 = (bf16[4,4,208,128]{3,2,1,0:T(8,128)(2,1)}, bf16[4,4,208,128]{3,2,1,0:T(8,128)(2,1)}, u32[]{:S(2)}, u32[]{:S(2)}) collective-permute-start(bf16[4,4,208,128]{3,2,1,0:T(8,128)(2,1)} %collective-permute-done.37.refs_3_), channel_id=1, source_target_pairs={{0,16},{1,17},{2,18},{3,19},{4,20},{5,21},{6,22},{7,23},{8,24},{9,... | collective-permute-start | bytes 2555912 | tf_op jit(solution)/shard_map/ppermute | solution.py:77
  322.5 22.5 %all-to-all-start.3 = ((bf16[16,192,128]{2,1,0:T(8,128)(2,1)}), bf16[16,192,128]{2,1,0:T(8,128)(2,1)}, u32[]{:S(2)}, u32[]{:S(2)}) async-start(bf16[16,192,128]{2,1,0:T(8,128)(2,1)} %copy-done.17), calls=%async_computation.3 | async-start | bytes 1572864 | tf_op jit(solution)/shard_map/all_to_all | solution.py:671
  (100 other events, 971.6 us)
Sparse Core Ops, SparseCore 0:
  10.8 68.8 all-gather.4
  82.3 68.0 all-gather.6
  249.6 85.5 all-reduce.3
